TPU v7x, 512 devices: a whole 4x8x8 slice. The times are simulated.
512 devices in a mesh: leaf: 32 (over x, z), rows: 16 (over y, core).
Axes of the slice: x: 4, y: 8, z: 8, core: 2. Of those that a mesh axis runs over, the one named last changes fastest.
Arguments:
- basis: bfloat16 [32, 16384, 256], P('leaf', 'rows'), may hold values from -0.046875 to 0.046875
- stiff: bfloat16 [32, 16384, 1664], P('leaf', 'rows'), may hold values from -6 to 6
- kcols: int32 [32, 256, 26], P('leaf', 'rows'), may hold values from 0 to 255
- couple: bfloat16 [32, 16384, 128], P('leaf', 'rows'), may hold values from -48 to 48
- links: int32 [32, 256, 2], P('leaf', 'rows'), may hold values from 0 to 15
- shift: float32 [32, 16384], P('leaf', 'rows'), may hold values from 1 to 10
- mass: float32 [32, 16384], P('leaf', 'rows'), may hold values from 0.5 to 4
Outputs:
- kred: float32 [32, 256, 1024], P('leaf', None, 'rows')
- mred: float32 [32, 256, 256], P('leaf', None, 'rows')
All inputs are finite; a program needn't handle non-finite values.
Results may differ from a plain program's by a relative error of at most 0.0028.
Values may be sent and summed in bfloat16 or wider, within the bound.
No kernel may reach another device: no remote copies, remote signals or barrier semaphores. Data moves between devices by JAX's collectives and lax.ppermute only.
A program may use at most 128 MiB of HBM per device.

v0:
```python
import jax
import jax.numpy as jnp
from jax import lax
from jax.sharding import PartitionSpec as P


def partner_2(value, axis, distance):
    mask = 2**distance
    pairs = [(source, source ^ mask) for source in range(lax.axis_size(axis))]
    return lax.ppermute(value, axis, pairs)


def block_apply(matrix, rows_in, nblocks, width):
    shaped = matrix.reshape(nblocks, matrix.shape[0] // nblocks, width)
    return lax.dot_general(
        shaped, rows_in, (((2,), (1,)), ((0,), (0,))), preferred_element_type=jnp.float32
    )


def shards(basis, stiff, kcols, couple, links, shift, mass):
    local_basis = basis[0]
    rows_local = local_basis.shape[0]
    modes = local_basis.shape[1]
    block = 64
    nblocks = rows_local // block
    width_all = stiff.shape[2]
    whole = lax.all_gather(local_basis, "rows", axis=0, tiled=True)
    sibling_basis = partner_2(local_basis, "leaf", 0)
    cousin_basis = partner_2(local_basis, "leaf", 1)
    table = whole.reshape(whole.shape[0] // block, block, modes)
    picked = jnp.take(table, kcols[0], axis=0).reshape(nblocks, width_all, modes)
    image = block_apply(stiff[0], picked, nblocks, width_all).reshape(rows_local, modes)
    image = (image + shift[0][:, None] * local_basis.astype(jnp.float32)).astype(jnp.bfloat16)
    terms = [jnp.dot(local_basis.T, image, preferred_element_type=jnp.float32)]
    for which, partner in ((0, sibling_basis), (1, cousin_basis)):
        partner_rows = jnp.take(partner.reshape(nblocks, block, modes), links[0][:, which], axis=0)
        cmat = couple[0][:, which * block : (which + 1) * block]
        coupled = (
            block_apply(cmat, partner_rows, nblocks, block)
            .reshape(rows_local, modes)
            .astype(jnp.bfloat16)
        )
        terms.append(jnp.dot(local_basis.T, coupled, preferred_element_type=jnp.float32))
    terms.append(jnp.zeros((modes, modes), jnp.float32))
    stacked = jnp.stack(terms)
    position = lax.axis_index("leaf") % 4
    order = jnp.bitwise_xor(jnp.arange(4, dtype=jnp.int32), position)
    row_block = jnp.take(stacked, order, axis=0).transpose(1, 0, 2).reshape(modes, 4 * modes)
    weighted = (mass[0][:, None] * local_basis.astype(jnp.float32)).astype(jnp.bfloat16)
    mass_block = jnp.dot(local_basis.T, weighted, preferred_element_type=jnp.float32)
    kred, mred = (
        lax.psum_scatter(row_block, "rows", scatter_dimension=1, tiled=True),
        lax.psum_scatter(mass_block, "rows", scatter_dimension=1, tiled=True),
    )
    return (kred[None], mred[None])


def solution(mesh):
    in_specs = (
        P("leaf", "rows", None),
        P("leaf", "rows", None),
        P("leaf", "rows", None),
        P("leaf", "rows", None),
        P("leaf", "rows", None),
        P("leaf", "rows"),
        P("leaf", "rows"),
    )
    out_specs = (P("leaf", None, "rows"), P("leaf", None, "rows"))
    return jax.shard_map(shards, mesh=mesh, in_specs=in_specs, out_specs=out_specs, check_vma=False)
```

profile of v0, /device:TPU:6, one launch (start us, length us, event | category | flops | bytes accessed | tf_op | source)
XLA Modules:
  0.0 202.7 jit_solution(15562521236871478926)
XLA Ops:
  8.0 6.2 %collective-permute-start.1 = (bf16[1024,256]{1,0:T(8,128)(2,1)}, bf16[1024,256]{1,0:T(8,128)(2,1)}, u32[]{:S(2)}, u32[]{:S(2)}) collective-permute-start(bf16[1024,256]{1,0:T(8,128)(2,1)} %bitcast.85), channel_id=1, source_target_pairs={{0,32},{16,48},{32,0},{48,16},{64,96},{80,112},{96,64},{112,80},{1... | collective-permute-start | bytes 1572872 | tf_op jit(solution)/shard_map/ppermute | solution.py:10
  14.2 4.3 %collective-permute-start = (bf16[1024,256]{1,0:T(8,128)(2,1)}, bf16[1024,256]{1,0:T(8,128)(2,1)}, u32[]{:S(2)}, u32[]{:S(2)}) collective-permute-start(bf16[1024,256]{1,0:T(8,128)(2,1)} %bitcast.86), channel_id=1, source_target_pairs={{0,16},{16,0},{32,48},{48,32},{64,80},{80,64},{96,112},{112,96},{1... | collective-permute-start | bytes 1572872 | tf_op jit(solution)/shard_map/ppermute | solution.py:10
  18.5 2.5 %convolution_bitcast_fusion.1 = f32[256,256]{0,1:T(8,128)} fusion(f32[1024]{0:T(1024)} %bitcast.98, bf16[1,1024,256]{2,1,0:T(8,128)(2,1)} %param.9), kind=kOutput, calls=%fused_computation.10 | convolution fusion | flops 135004160 | bytes 790528 | tf_op jit(solution)/shard_map/dot_general | solution.py:50
  21.0 0.7 compare_and_fusion
  21.7 0.7 compare_select_fusion
  22.4 0.8 compare_and_fusion.2
  24.2 1.3 reduce.3
  25.7 1.9 fusion.19
  27.6 10.2 %collective-permute-done.1 = bf16[1024,256]{1,0:T(8,128)(2,1)} collective-permute-done((bf16[1024,256]{1,0:T(8,128)(2,1)}, bf16[1024,256]{1,0:T(8,128)(2,1)}, u32[]{:S(2)}, u32[]{:S(2)}) %collective-permute-start.1) | collective-permute-done | bytes 524320 | tf_op jit(solution)/shard_map/ppermute | solution.py:10
  37.8 2.4 %gather_fusion.3 = bf16[16,64,256]{2,1,0:T(8,128)(2,1)} fusion(bf16[16,64,256]{2,1,0:T(8,128)(2,1)} %bitcast.21, s32[1024]{0:T(1024)S(1)} %pad_clamp_fusion.1), kind=kCustom, calls=%fused_computation.1.clone | custom fusion | bytes 1048640 | tf_op jit(solution)/shard_map/jit(_take)/gather | solution.py:36
  40.2 1.5 convolution_convert_fusion
  41.7 2.1 %convolution_bitcast_fusion.2 = f32[1,256,256]{1,2,0:T(8,128)} fusion(bf16[1024,256]{1,0:T(8,128)(2,1)S(1)} %bitcast.90, bf16[1,1024,256]{2,1,0:T(8,128)(2,1)} %param.9), kind=kOutput, calls=%fused_computation.11 | convolution fusion | flops 134217728 | bytes 1310720 | tf_op jit(solution)/shard_map/dot_general | solution.py:43
  43.8 2.5 %gather_fusion.2 = bf16[16,64,256]{2,1,0:T(8,128)(2,1)} fusion(bf16[16,64,256]{2,1,0:T(8,128)(2,1)} %bitcast.13, s32[1024]{0:T(1024)S(1)} %pad_clamp_fusion.2), kind=kCustom, calls=%fused_computation.clone | custom fusion | bytes 1048640 | tf_op jit(solution)/shard_map/jit(_take)/gather | solution.py:36
  46.2 1.5 convolution_convert_fusion.1
  47.7 2.1 %convolution_bitcast_fusion.3 = f32[1,256,256]{1,2,0:T(8,128)} fusion(bf16[1024,256]{1,0:T(8,128)(2,1)S(1)} %bitcast.91, bf16[1,1024,256]{2,1,0:T(8,128)(2,1)} %param.9), kind=kOutput, calls=%fused_computation.12 | convolution fusion | flops 134217728 | bytes 1310720 | tf_op jit(solution)/shard_map/dot_general | solution.py:43
  49.8 23.2 %all-gather.3.cloned.1.call-done = bf16[1,16384,256]{2,1,0:T(8,128)(2,1)} async-done(((bf16[1,1024,256]{2,1,0:T(8,128)(2,1)}), bf16[1,16384,256]{2,1,0:T(8,128)(2,1)}) %all-gather.3.cloned.1.call-update) | async-done | bytes 8388624 | tf_op jit(solution)/shard_map/all_gather | solution.py:27
  73.0 16.5 %gather_fusion = bf16[416,64,256]{2,1,0:T(8,128)(2,1)} fusion(bf16[256,64,256]{2,1,0:T(8,128)(2,1)} %bitcast.84, s32[1024]{0:T(1024)S(1)} %pad_clamp_fusion.3), kind=kCustom, calls=%fused_computation.2 | custom fusion | bytes 27264640 | tf_op jit(solution)/shard_map/jit(_take)/gather | solution.py:31
  89.4 7.4 %bitcast_select_fusion = bf16[16,1664,256]{2,1,0:T(8,128)(2,1)S(1)} fusion(pred[16,1664]{1,0:T(8,128)(4,1)S(1)} %broadcast_in_dim.41, bf16[16,1664,256]{2,1,0:T(8,128)(2,1)} %bitcast.83), kind=kLoop, calls=%fused_computation.4 | loop fusion | flops 6815744 | bytes 27289600 | tf_op jit(solution)/shard_map/jit(_take)/select_n | solution.py:31
  96.9 2.4 %fusion.1 = bf16[16,64,256]{2,1,0:T(8,128)(2,1)S(1)} fusion(bf16[16,64,1664]{2,1,0:T(8,128)(2,1)S(1)} %bitcast.82, bf16[16,1664,256]{2,1,0:T(8,128)(2,1)S(1)} %bitcast_select_fusion, f32[16,64]{1,0:T(8,128)S(1)} %mul.20, bf16[16,64,256]{2,1,0:T(8,128)(2,1)S(1)} %bitcast.87), kind=kOutput, calls=%fused_computation.7 | convolution fusion | flops 873463808 | bytes 18092032 | tf_op jit(solution)/shard_map/dot_general | solution.py:15
  99.7 1.1 maximum_maximum_fusion
  100.8 2.9 %gather_fusion.1 = f32[4,256,256]{1,2,0:T(8,128)} fusion(f32[4,256,256]{1,2,0:T(8,128)} %maximum_maximum_fusion, s32[1024]{0:T(1024)S(1)} %pad_clamp_fusion), kind=kCustom, calls=%fused_computation.3 | custom fusion | bytes 2097168 | tf_op jit(solution)/shard_map/jit(_take)/gather | solution.py:48
  103.7 2.4 %broadcast_select_fusion = f32[4,256,256]{1,2,0:T(8,128)} fusion(f32[4,256,256]{1,2,0:T(8,128)} %gather_fusion.1, pred[4]{0:T(512)(128)(4,1)S(1)} %compare_and_fusion.3), kind=kLoop, calls=%fused_computation.20 | loop fusion | flops 262144 | bytes 2097156 | tf_op jit(solution)/shard_map/jit(_take)/select_n | solution.py:48
  106.1 27.7 %reduce-scatter.5.cloned.1.call-done = f32[256,16]{0,1:T(8,128)} async-done(((f32[256,256]{0,1:T(8,128)}), f32[256,16]{0,1:T(8,128)}) %reduce-scatter.5.cloned.1.call-update) | async-done | bytes 16400 | tf_op jit(solution)/shard_map/reduce_scatter | solution.py:53
  133.8 62.4 %reduce-scatter.3.cloned.1.call-done = f32[256,64]{0,1:T(8,128)} async-done(((f32[256,1024]{0,1:T(8,128)}), f32[256,64]{0,1:T(8,128)}) %reduce-scatter.3.cloned.1.call-update) | async-done | bytes 65552 | tf_op jit(solution)/shard_map/reduce_scatter | solution.py:52
  (28 shorter events, 2.3 us)
Async XLA Ops:
  7.2 89.7 %copy-start = (bf16[1,1024,1664]{2,1,0:T(8,128)(2,1)S(1)}, bf16[1,1024,1664]{2,1,0:T(8,128)(2,1)}, u32[]{:S(2)}) copy-start(bf16[1,1024,1664]{2,1,0:T(8,128)(2,1)} %param.10) | copy-start | bytes 10223620
  7.2 65.8 %all-gather.3.cloned.1.call-start = ((), (), s32[]{:S(2)}) async-start(), calls=%async_computation.4 | async-start | bytes 8912896 | tf_op jit(solution)/shard_map/all_gather | solution.py:27
  7.9 125.9 %reduce-scatter.5.cloned.1.call-start = ((), (), s32[]{:S(2)}) async-start(), calls=%async_computation.3 | async-start | bytes 278528 | tf_op jit(solution)/shard_map/reduce_scatter | solution.py:53
  8.0 29.8 %collective-permute-start.1 = (bf16[1024,256]{1,0:T(8,128)(2,1)}, bf16[1024,256]{1,0:T(8,128)(2,1)}, u32[]{:S(2)}, u32[]{:S(2)}) collective-permute-start(bf16[1024,256]{1,0:T(8,128)(2,1)} %bitcast.85), channel_id=1, source_target_pairs={{0,32},{16,48},{32,0},{48,16},{64,96},{80,112},{96,64},{112,80},{1... | collective-permute-start | bytes 1572872 | tf_op jit(solution)/shard_map/ppermute | solution.py:10
  14.2 29.6 %collective-permute-start = (bf16[1024,256]{1,0:T(8,128)(2,1)}, bf16[1024,256]{1,0:T(8,128)(2,1)}, u32[]{:S(2)}, u32[]{:S(2)}) collective-permute-start(bf16[1024,256]{1,0:T(8,128)(2,1)} %bitcast.86), channel_id=1, source_target_pairs={{0,16},{16,0},{32,48},{48,32},{64,80},{80,64},{96,112},{112,96},{1... | collective-permute-start | bytes 1572872 | tf_op jit(solution)/shard_map/ppermute | solution.py:10
  21.0 175.2 %reduce-scatter.3.cloned.1.call-start = ((), (), s32[]{:S(2)}) async-start(), calls=%async_computation.2 | async-start | bytes 1114112 | tf_op jit(solution)/shard_map/reduce_scatter | solution.py:52
  89.4 7.5 %copy-start.1 = (bf16[1,1024,256]{2,1,0:T(8,128)(2,1)S(1)}, bf16[1,1024,256]{2,1,0:T(8,128)(2,1)}, u32[]{:S(2)}) copy-start(bf16[1,1024,256]{2,1,0:T(8,128)(2,1)} %param.9) | copy-start | bytes 1572868
  96.9 2.8 %copy-start.2 = (f32[1,256,256]{1,2,0:T(8,128)S(1)}, f32[1,256,256]{1,2,0:T(8,128)}, u32[]{:S(2)}) copy-start(f32[1,256,256]{1,2,0:T(8,128)} %convolution_bitcast_fusion.2) | copy-start | bytes 786436
  96.9 2.8 %copy-start.3 = (f32[1,256,256]{1,2,0:T(8,128)S(1)}, f32[1,256,256]{1,2,0:T(8,128)}, u32[]{:S(2)}) copy-start(f32[1,256,256]{1,2,0:T(8,128)} %convolution_bitcast_fusion.3) | copy-start | bytes 786436
Sparse Core Ops, SparseCore 0:
  10.1 62.8 all-gather.2
  76.3 57.4 reduce-scatter.4
  137.4 58.6 reduce-scatter.2
where the time goes:
time: 203 us
  waiting for transfers between devices  124 us (61%)
  local copies, waits for them, and re-layouts  27.2 us (13%)
  other arithmetic  14.5 us (7%)
  between operations  13.9 us (7%)
  matrix products  12.4 us (6%)
  starting transfers between devices  10.6 us (5%)
    reduce_scatter x1, waiting for transfers between devices, shards(): lax.psum_scatter(row_block, 'rows', scatter_dimension=1, tiled=True)  62.4 us
    reduce_scatter x1, waiting for transfers between devices, shards(): lax.psum_scatter(mass_block, 'rows', scatter_dimension=1, tiled=True)  27.7 us
    all_gather x1, waiting for transfers between devices, shards(): whole = lax.all_gather(local_basis, 'rows', axis=0, tiled=True)  23.2 us
    gather x1, local copies, waits for them, and re-layouts, shards(): jnp.take(table, kcols[0], axis=0).reshape(nblocks, width_all, modes)  16.5 us
    ppermute x2, starting transfers between devices, partner_2(): return lax.ppermute(value, axis, pairs)  10.5 us
    ppermute x2, waiting for transfers between devices, partner_2(): return lax.ppermute(value, axis, pairs)  10.2 us
    select_n x2, other arithmetic, shards(): jnp.take(table, kcols[0], axis=0).reshape(nblocks, width_all, modes)  8.14 us
    dot_general x3, matrix products, block_apply(): lax.dot_general(shaped, rows_in, (((2,), (1,)), ((0,), (0,))), preferred_...  5.38 us
  transfers between devices with their start and end apart: 5, of which 4 were waited for; matrix products, arithmetic and copies ran while one was open for 27% of the time, Pallas kernels for 0%

commit v1 on v0

v1 whole, which is shorter than its diff:
```python
import functools

import jax
import jax.numpy as jnp
from jax import lax
from jax.experimental import pallas as pl
from jax.experimental.pallas import tpu as pltpu
from jax.sharding import PartitionSpec as P

F32, BF16 = jnp.float32, jnp.bfloat16
BLK = 64
MIB = 2**20
COUPLE, SHIFT, MASS, KCOLS, LINKS, AUX = 0, 1024, 1032, 1040, 1056, 1072
VMEM = pl.BlockSpec(memory_space=pltpu.VMEM)
SMEM = pl.BlockSpec(memory_space=pltpu.SMEM)
ANY = pl.BlockSpec(memory_space=pl.ANY)
HBM = pl.BlockSpec(memory_space=pltpu.HBM)


def place():
    row = lax.axis_index("rows")
    return row // 4, (row // 2) % 2, row % 2


def send(value, to):
    leaves, rows = lax.axis_size("leaf"), lax.axis_size("rows")
    pairs = []
    for leaf in range(leaves):
        for row in range(rows):
            target = to(leaf, row)
            if target is not None:
                pairs.append((leaf * rows + row, target[0] * rows + target[1]))
    return lax.ppermute(value, ("leaf", "rows"), pairs)


def to_core(leaf, row):
    return leaf, row ^ 1


def to_side(leaf, row):
    return leaf, row ^ 2


def ring(forward):
    def to(leaf, row):
        step = 2 if (row % 2 == 0) == forward else -2
        return leaf, (row + step) % 16

    return to


def to_group(mask):
    return lambda leaf, row: (leaf, row ^ (4 * mask))


def to_own_group(mask):
    def to(leaf, row):
        return (leaf, 4 * (leaf % 4) + row % 4) if row // 4 == (leaf % 4) ^ mask else None

    return to


def call(body, outs, arrays, far=(), scratch=(), flops=0, vmem=8, aliases=None):
    moved = sum(x.size * x.dtype.itemsize for x in [*arrays, *far, *outs])
    return pl.pallas_call(
        body,
        out_shape=outs,
        in_specs=[VMEM] * len(arrays) + [HBM] * len(far),
        out_specs=[VMEM] * len(outs),
        scratch_shapes=list(scratch),
        input_output_aliases=aliases or {},
        compiler_params=pltpu.CompilerParams(vmem_limit_bytes=vmem * MIB),
        cost_estimate=pl.CostEstimate(flops=flops, bytes_accessed=moved, transcendentals=0),
    )(*arrays, *far)


def fetch(pairs, sems):
    copies = [pltpu.make_async_copy(src, dst, sems.at[n]) for n, (src, dst) in enumerate(pairs)]
    for copy in copies:
        copy.start()
    return copies


def shape(*dims, dtype=F32):
    return jax.ShapeDtypeStruct(dims, dtype)


def mine_of(width, column):
    here = lax.broadcasted_iota(jnp.int32, (width, 128), 0)
    want = column(lax.broadcasted_iota(jnp.int32, (width, 128), 1))
    return (here == want).astype(F32).astype(BF16)


def dot(a, b):
    return jnp.dot(a, b, preferred_element_type=F32)


def dot_t(a, b):
    return lax.dot_general(a, b, (((0,), (0,)), ((), ())), preferred_element_type=F32)


def after(value, *others):
    return lax.optimization_barrier((value, *others))[0]


def aux_kernel(couple_at, kcols_at, links_at, shift_at, mass_at, out, couple, kcols, links, shift, mass, sems):
    held = (couple, kcols, links, shift, mass)
    for copy in fetch(zip((couple_at, kcols_at, links_at, shift_at, mass_at), held), sems):
        copy.wait()
    out[COUPLE : COUPLE + 1024, :] = couple[0].astype(F32)
    for k in range(8):
        out[SHIFT + k : SHIFT + k + 1, :] = shift[:, k * 128 : (k + 1) * 128]
        out[MASS + k : MASS + k + 1, :] = mass[:, k * 128 : (k + 1) * 128]
    out[KCOLS:AUX, :] = jnp.zeros((AUX - KCOLS, 128), F32)
    out[KCOLS : KCOLS + 16, 0:26] = kcols[0].astype(F32)
    out[LINKS : LINKS + 2, 0:16] = links[0].astype(F32)


def half_kernel(own, other, out, both):
    _, _, core = place()
    pick = mine_of(256, lambda n: 64 * core + n + jnp.where(n >= 64, 64, 0))
    out[pl.ds(pl.multiple_of(core * 1024, 1024), 1024), :] = dot(own[...], pick).astype(BF16)
    out[pl.ds(pl.multiple_of((1 - core) * 1024, 1024), 1024), :] = dot(other[...], pick).astype(BF16)
    both[0:1024, :] = own[...]
    both[1024:2048, :] = other[...]


def spread(dst, rows_own, rows_other):
    for part, rows in enumerate((rows_own, rows_other)):
        turned = jnp.transpose(jnp.concatenate([rows, jnp.zeros((120, 128), F32)], axis=0))
        for k in range(8):
            dst[part * 1024 + k * 128 : part * 1024 + (k + 1) * 128, :] = jnp.broadcast_to(
                turned[:, k : k + 1], (128, 128)
            )


def early_kernel(both, aux, aux_other, partner, to_send, to_keep, mred, coupled, weights, masked, spots, at, sem):
    _, _, core = place()
    spots[...] = jnp.zeros((8, 128), jnp.int32)
    for part, rows in enumerate((aux, aux_other)):
        links = rows[LINKS : LINKS + 2, 0:16].astype(jnp.int32)
        spots[part : part + 1, 0:16] = part * 1024 + jnp.where(core == 0, links[0:1, :], links[1:2, :]) * BLK
    copy = pltpu.make_async_copy(spots, at, sem)
    copy.start()
    mine = lax.broadcasted_iota(jnp.int32, (1024, 128), 1) // BLK == core
    for part, rows in enumerate((aux, aux_other)):
        couple = rows[COUPLE : COUPLE + 1024, :]
        masked[part * 1024 : (part + 1) * 1024, :] = jnp.where(mine, couple, 0.0).astype(BF16)
    copy.wait()

    def one(b, carry):
        rows = pl.ds(pl.multiple_of(b * BLK, BLK), BLK)
        block = partner[pl.ds(pl.multiple_of(at[b // 16, b % 16], BLK), BLK), :]
        coupled[rows, :] = dot(masked[rows, :], jnp.concatenate([block, block], axis=0)).astype(BF16)
        return carry

    lax.fori_loop(0, 32, one, 0, unroll=8)
    spread(weights, aux[MASS : MASS + 8, :], aux_other[MASS : MASS + 8, :])
    pick = mine_of(256, lambda n: 64 * ((n % 64) // 16) + 32 * (n // 64) + 16 * core + n % 16)
    weighted = (weights[...] * dot(both[...], pick)).astype(BF16)
    mred[...] = dot_t(weighted, both[...])
    term = dot_t(coupled[...], both[...])
    for k in range(2):
        low, high = term[k * 128 : k * 128 + 64, :], term[k * 128 + 64 : k * 128 + 128, :]
        to_keep[k * 64 : (k + 1) * 64, :] = jnp.where(core == 0, low, high)
        to_send[k * 64 : (k + 1) * 64, :] = jnp.where(core == 0, high, low)


def turn_kernel(kept, came, mred, to_send, to_keep):
    _, side, core = place()
    sib = jnp.where(core == 0, kept[...], came[...])
    cous = jnp.where(core == 0, came[...], kept[...])
    for t, term in enumerate((sib, cous, mred[...])):
        low, high = term[0:64, :], term[64:128, :]
        to_send[t * 64 : (t + 1) * 64, :] = jnp.where(side == 0, high, low)
        to_keep[t * 64 : (t + 1) * 64, :] = jnp.where(side == 0, low, high)


def split_kernel(kept, came, to_send, to_keep):
    group, _, _ = place()
    odd = (group ^ (lax.axis_index("leaf") % 4)) % 2 == 1
    sib = kept[0:64, :] + came[0:64, :]
    cous = kept[64:128, :] + came[64:128, :]
    mass = kept[128:192, :] + came[128:192, :]
    to_keep[0:64, :] = jnp.where(odd, sib, cous)
    to_send[0:64, :] = jnp.where(odd, cous, sib)
    low = group % 2 == 0
    for k in range(2):
        even, uneven = mass[k * 32 : k * 32 + 16, :], mass[k * 32 + 16 : k * 32 + 32, :]
        to_keep[64 + k * 16 : 80 + k * 16, :] = jnp.where(low, even, uneven)
        to_send[64 + k * 16 : 80 + k * 16, :] = jnp.where(low, uneven, even)


def stage_kernel(both, aux, aux_other, *refs):
    kcols_at, stiff, stiff_other = refs[:3]
    pieces = refs[3:10]
    table, matrix, start, spots, kcols, sems = refs[10:]
    _, _, core = place()
    chip = lax.axis_index("rows") // 2
    places = [2048 * d for d in (0, 7, 1, 6, 2, 5, 3)]
    pairs = [(kcols_at, kcols), (pieces[0], table.at[0:2048, :])]
    pairs += [(piece, table.at[lo : lo + 2048, :]) for piece, lo in list(zip(pieces, places))[1:]]
    pairs += [(stiff.at[0], matrix.at[0:1024, :]), (stiff_other, matrix.at[1024:2048, :])]
    copies = fetch(pairs, sems)
    spread(start, aux[SHIFT : SHIFT + 8, :], aux_other[SHIFT : SHIFT + 8, :])
    copies[0].wait()
    copies[1].wait()
    spots[...] = jnp.zeros((32, 128), jnp.int32)
    for part in range(2):
        column = kcols[0] if part == 0 else aux_other[KCOLS : KCOLS + 16, 0:26].astype(jnp.int32)
        ahead = column // 32 - chip
        ahead = jnp.where(core == 0, ahead, -ahead) & 7
        spots[part * 16 : (part + 1) * 16, 0:26] = ahead * 2048 + (column % 32) * BLK
    for part in range(2):
        rows = slice(part * 1024, (part + 1) * 1024)
        mine = pl.ds(pl.multiple_of((part * 1024 + core * 1024) % 2048, 1024), 1024)
        start[rows, :] = start[rows, :] * table[mine, :].astype(F32)
    for copy in copies[2:]:
        copy.wait()


def own_kernel(table, matrix, start, spots, both, last_at, to_send, to_keep, full, image, at, sems):
    _, side, _ = place()
    copies = fetch([(spots, at), (last_at, full.at[4 * 2048 : 5 * 2048, :])], sems)
    for copy in copies:
        copy.wait()

    def one(b, carry):
        rows = pl.ds(pl.multiple_of(b * BLK, BLK), BLK)
        total = start[rows, :]
        blocks = [full[pl.ds(pl.multiple_of(at[b, k], BLK), BLK), :] for k in range(26)]
        for g in range(0, 26, 4):
            picked = jnp.concatenate(blocks[g : g + 4], axis=0)
            width = picked.shape[0]
            total += dot(matrix[rows, g * BLK : g * BLK + width], picked)
        image[rows, :] = total.astype(BF16)
        return carry

    lax.fori_loop(0, 32, one, 0, unroll=8)
    result = dot_t(image[...], both[...])
    low, high = result[0:64, :], result[64:128, :]
    to_send[...] = jnp.where(side == 0, high, low)
    to_keep[...] = jnp.where(side == 0, low, high)


def gather_kernel(kept, came, early_kept, early_came, total, pay, base, mass_base):
    group, _, _ = place()
    term = group ^ (lax.axis_index("leaf") % 4)
    own = kept[...] + came[...]
    early = early_kept[0:64, :] + early_came[0:64, :]
    total[...] = own
    zero = jnp.zeros_like(own)
    pay[0:64, :] = jnp.where(term == 2, own, jnp.where(term == 1, zero, early))
    base[...] = jnp.where(term == 0, own, jnp.where(term == 3, zero, early))
    first = early_kept[64:80, :] + early_came[64:80, :]
    second = early_kept[80:96, :] + early_came[80:96, :]
    low = group < 2
    pay[64:80, :] = jnp.where(low, second, first)
    mass_base[...] = jnp.where(low, first, second)


def last_kernel(base, mass_base, one, two, three, kred, mred):
    kred[...] = base[...] + one[...] + two[0:64, :] + three[...]
    mred[...] = mass_base[...] + two[64:80, :]


def shards(basis, stiff, kcols, couple, links, shift, mass):
    own = basis[0]
    links = links.transpose(0, 2, 1)
    other = send(own, to_core)
    half, both = call(half_kernel, [shape(2048, 128, dtype=BF16), shape(2048, 256, dtype=BF16)], [own, other])
    left1 = send(half, ring(True))
    (aux,) = call(
        aux_kernel,
        [shape(AUX, 128)],
        [],
        [couple, after(kcols, half), links, shift, mass],
        [
            pltpu.VMEM((1, 1024, 128), BF16),
            pltpu.VMEM((1, 16, 26), jnp.int32),
            pltpu.VMEM((1, 2, 16), jnp.int32),
            pltpu.VMEM((1, 1024), F32),
            pltpu.VMEM((1, 1024), F32),
            pltpu.SemaphoreType.DMA((5,)),
        ],
    )
    right1 = send(after(half, aux), ring(False))
    partner = send(both, lambda leaf, row: (leaf ^ (1 + row % 2), row))
    stiff_other = send(stiff[0], to_core)
    aux_other = send(after(aux, stiff_other), to_core)
    left2, right2 = send(left1, ring(True)), send(right1, ring(False))
    left3, right3 = send(left2, ring(True)), send(right2, ring(False))
    left4 = send(left3, ring(True))
    go, keep, mass_part = call(
        early_kernel,
        [shape(128, 256)] * 3,
        [both, aux, aux_other, partner],
        [],
        [
            pltpu.VMEM((2048, 256), BF16),
            pltpu.VMEM((2048, 128), F32),
            pltpu.VMEM((2048, 128), BF16),
            pltpu.VMEM((8, 128), jnp.int32),
            pltpu.SMEM((8, 128), jnp.int32),
            pltpu.SemaphoreType.DMA,
        ],
        flops=2**30,
        vmem=16,
    )
    came = send(go, to_core)
    go, keep = call(turn_kernel, [shape(192, 256)] * 2, [keep, came, mass_part])
    came = send(go, to_side)
    go, early_keep = call(split_kernel, [shape(96, 256)] * 2, [keep, came])
    early_came = send(go, to_group(1))

    table, matrix, start, spots = call(
        stage_kernel,
        [shape(16384, 128, dtype=BF16), shape(2048, 1664, dtype=BF16), shape(2048, 128), shape(32, 128, dtype=jnp.int32)],
        [both, aux, aux_other],
        [kcols, stiff, stiff_other, half, left1, right1, left2, right2, left3, right3],
        [pltpu.VMEM((1, 16, 26), jnp.int32), pltpu.SemaphoreType.DMA((10,))],
    )
    go, keep, _ = call(
        own_kernel,
        [shape(64, 256), shape(64, 256), shape(16384, 128, dtype=BF16)],
        [table, matrix, start, spots, both],
        [left4],
        [pltpu.VMEM((2048, 128), BF16), pltpu.SMEM((32, 128), jnp.int32), pltpu.SemaphoreType.DMA((2,))],
        flops=2**30,
        aliases={0: 2},
    )
    came = send(go, to_side)
    total, pay, base, mass_base = call(
        gather_kernel,
        [shape(64, 256), shape(80, 256), shape(64, 256), shape(16, 256)],
        [keep, came, early_keep, early_came],
    )
    one = send(total, to_own_group(1))
    three = send(total, to_own_group(3))
    two = send(pay, to_group(2))
    kred, mred = call(last_kernel, [shape(64, 256), shape(16, 256)], [base, mass_base, one, two, three])
    return (kred.T[None], mred.T[None])


def solution(mesh):
    in_specs = (
        P("leaf", "rows", None),
        P("leaf", "rows", None),
        P("leaf", "rows", None),
        P("leaf", "rows", None),
        P("leaf", "rows", None),
        P("leaf", "rows"),
        P("leaf", "rows"),
    )
    out_specs = (P("leaf", None, "rows"), P("leaf", None, "rows"))
    return jax.shard_map(shards, mesh=mesh, in_specs=in_specs, out_specs=out_specs, check_vma=False)
```

time: 203 us -> 110 us (0.54)
  the two profiles are of different devices: /device:TPU:6 before, /device:TPU:8 now
where the time goes in v1:
time: 110 us; the launch traced here: 109 us
  starting transfers between devices  60.9 us (55%)
  waiting for transfers between devices  32.3 us (29%)
  Pallas kernels  9.86 us (9%)
  local copies, waits for them, and re-layouts  4.74 us (4%)
    ppermute x18, starting transfers between devices, send(): return lax.ppermute(value, ('leaf', 'rows'), pairs)  60.9 us
    ppermute x18, waiting for transfers between devices, send(): return lax.ppermute(value, ('leaf', 'rows'), pairs)  32.3 us
    pallas_call x9, Pallas kernels, call(): pl.pallas_call(body, out_shape=outs, in_specs=[VMEM] * len(arrays) + [HBM...  9.86 us
    unnamed x16, local copies, waits for them, and re-layouts  4.74 us
  transfers between devices with their start and end apart: 18, of which 9 were waited for; matrix products, arithmetic and copies ran while one was open for 0% of the time, Pallas kernels for 8%

profile of v1, /device:TPU:8, one launch (start us, length us, event | category | flops | bytes accessed | tf_op | source)
XLA Modules:
  0.0 108.7 jit_solution(2429010375309352378)
XLA Ops:
  0.6 2.2 %collective-permute-start.1 = (bf16[1024,1664]{1,0:T(8,128)(2,1)}, bf16[1024,1664]{1,0:T(8,128)(2,1)S(1)}, u32[]{:S(2)}, u32[]{:S(2)}) collective-permute-start(bf16[1024,1664]{1,0:T(8,128)(2,1)} %bitcast.9), channel_id=1, source_target_pairs={{0,1},{1,0},{2,3},{3,2},{4,5},{5,4},{6,7},{7,6},{8,9},{9,8},{10,11... | collective-permute-start | bytes 10223624 | tf_op jit(solution)/shard_map/ppermute | solution.py:33
  2.8 2.4 %collective-permute-start = (bf16[1024,256]{1,0:T(8,128)(2,1)}, bf16[1024,256]{1,0:T(8,128)(2,1)S(1)}, u32[]{:S(2)}, u32[]{:S(2)}) collective-permute-start(bf16[1024,256]{1,0:T(8,128)(2,1)} %bitcast.10), channel_id=1, source_target_pairs={{0,1},{1,0},{2,3},{3,2},{4,5},{5,4},{6,7},{7,6},{8,9},{9,8},{10,11... | collective-permute-start | bytes 1572872 | tf_op jit(solution)/shard_map/ppermute | solution.py:33
  5.2 4.5 %collective-permute-done.other = bf16[1024,256]{1,0:T(8,128)(2,1)S(1)} collective-permute-done((bf16[1024,256]{1,0:T(8,128)(2,1)}, bf16[1024,256]{1,0:T(8,128)(2,1)S(1)}, u32[]{:S(2)}, u32[]{:S(2)}) %collective-permute-start) | collective-permute-done | bytes 524320 | tf_op jit(solution)/shard_map/ppermute | solution.py:33
  11.3 3.5 %collective-permute-start.3 = (bf16[2048,128]{1,0:T(8,128)(2,1)S(1)}, bf16[2048,128]{1,0:T(8,128)(2,1)S(1)}, u32[]{:S(2)}, u32[]{:S(2)}) collective-permute-start(bf16[2048,128]{1,0:T(8,128)(2,1)S(1)} %get-tuple-element.30.refs_3_), channel_id=1, source_target_pairs={{0,2},{1,15},{2,4},{3,1},{4,6},{5,3},{6,8},{7,5},{8,10},{9,7},{10,... | collective-permute-start | bytes 1572872 | tf_op jit(solution)/shard_map/ppermute | solution.py:33
  18.6 6.2 %collective-permute-start.4 = (bf16[2048,128]{1,0:T(8,128)(2,1)S(1)}, bf16[2048,128]{1,0:T(8,128)(2,1)S(1)}, u32[]{:S(2)}, u32[]{:S(2)}) collective-permute-start(bf16[2048,128]{1,0:T(8,128)(2,1)S(1)} %get-tuple-element.30.refs_3_), channel_id=1, source_target_pairs={{0,14},{1,3},{2,0},{3,5},{4,2},{5,7},{6,4},{7,9},{8,6},{9,11},{10,... | collective-permute-start | bytes 1572872 | tf_op jit(solution)/shard_map/ppermute | solution.py:33
  28.1 2.5 %collective-permute-start.11 = (bf16[2048,256]{1,0:T(8,128)(2,1)S(1)}, bf16[2048,256]{1,0:T(8,128)(2,1)S(1)}, u32[]{:S(2)}, u32[]{:S(2)}) collective-permute-start(bf16[2048,256]{1,0:T(8,128)(2,1)S(1)} %get-tuple-element.26.both), channel_id=1, source_target_pairs={{0,16},{1,33},{2,18},{3,35},{4,20},{5,37},{6,22},{7,39},{8,24},{9,... | collective-permute-start | bytes 3145736 | tf_op jit(solution)/shard_map/ppermute | solution.py:33
  30.6 2.8 %collective-permute-done.4.refs_5_ = bf16[2048,128]{1,0:T(8,128)(2,1)S(1)} collective-permute-done((bf16[2048,128]{1,0:T(8,128)(2,1)S(1)}, bf16[2048,128]{1,0:T(8,128)(2,1)S(1)}, u32[]{:S(2)}, u32[]{:S(2)}) %collective-permute-start.4) | collective-permute-done | bytes 524320 | tf_op jit(solution)/shard_map/ppermute | solution.py:33
  33.4 7.1 %collective-permute-start.6 = (bf16[2048,128]{1,0:T(8,128)(2,1)S(1)}, bf16[2048,128]{1,0:T(8,128)(2,1)S(1)}, u32[]{:S(2)}, u32[]{:S(2)}) collective-permute-start(bf16[2048,128]{1,0:T(8,128)(2,1)S(1)} %collective-permute-done.4.refs_5_), channel_id=1, source_target_pairs={{0,14},{1,3},{2,0},{3,5},{4,2},{5,7},{6,4},{7,9},{8,6},{9,11},{10,... | collective-permute-start | bytes 1572872 | tf_op jit(solution)/shard_map/ppermute | solution.py:33
  40.6 1.9 %collective-permute-start.7 = (bf16[2048,128]{1,0:T(8,128)(2,1)S(1)}, bf16[2048,128]{1,0:T(8,128)(2,1)S(1)}, u32[]{:S(2)}, u32[]{:S(2)}) collective-permute-start(bf16[2048,128]{1,0:T(8,128)(2,1)S(1)} %collective-permute-done.5.refs_6_), channel_id=1, source_target_pairs={{0,2},{1,15},{2,4},{3,1},{4,6},{5,3},{6,8},{7,5},{8,10},{9,7},{10,... | collective-permute-start | bytes 1572872 | tf_op jit(solution)/shard_map/ppermute | solution.py:33
  42.5 1.9 %collective-permute-start.2 = (f32[1072,128]{1,0:T(8,128)S(1)}, f32[1072,128]{1,0:T(8,128)S(1)}, u32[]{:S(2)}, u32[]{:S(2)}) collective-permute-start(f32[1072,128]{1,0:T(8,128)S(1)} %shard_map.87.aux), channel_id=1, source_target_pairs={{0,1},{1,0},{2,3},{3,2},{4,5},{5,4},{6,7},{7,6},{8,9},{9,8},{10,11... | collective-permute-start | bytes 1646600 | tf_op jit(solution)/shard_map/ppermute | solution.py:33
  44.4 7.6 %collective-permute-done.6.refs_7_ = bf16[2048,128]{1,0:T(8,128)(2,1)S(1)} collective-permute-done((bf16[2048,128]{1,0:T(8,128)(2,1)S(1)}, bf16[2048,128]{1,0:T(8,128)(2,1)S(1)}, u32[]{:S(2)}, u32[]{:S(2)}) %collective-permute-start.6) | collective-permute-done | bytes 524320 | tf_op jit(solution)/shard_map/ppermute | solution.py:33
  52.1 5.9 %collective-permute-start.8 = (bf16[2048,128]{1,0:T(8,128)(2,1)S(1)}, bf16[2048,128]{1,0:T(8,128)(2,1)S(1)}, u32[]{:S(2)}, u32[]{:S(2)}) collective-permute-start(bf16[2048,128]{1,0:T(8,128)(2,1)S(1)} %collective-permute-done.6.refs_7_), channel_id=1, source_target_pairs={{0,14},{1,3},{2,0},{3,5},{4,2},{5,7},{6,4},{7,9},{8,6},{9,11},{10,... | collective-permute-start | bytes 1572872 | tf_op jit(solution)/shard_map/ppermute | solution.py:33
  58.0 1.9 %collective-permute-start.9 = (bf16[2048,128]{1,0:T(8,128)(2,1)S(1)}, bf16[2048,128]{1,0:T(8,128)(2,1)S(1)}, u32[]{:S(2)}, u32[]{:S(2)}) collective-permute-start(bf16[2048,128]{1,0:T(8,128)(2,1)S(1)} %collective-permute-done.7.refs_8_), channel_id=1, source_target_pairs={{0,2},{1,15},{2,4},{3,1},{4,6},{5,3},{6,8},{7,5},{8,10},{9,7},{10,... | collective-permute-start | bytes 1572872 | tf_op jit(solution)/shard_map/ppermute | solution.py:33
  60.0 2.9 %shard_map.90 = (f32[128,256]{1,0:T(8,128)S(1)}, f32[128,256]{1,0:T(8,128)S(1)}, f32[128,256]{1,0:T(8,128)S(1)}) custom-call(bf16[2048,256]{1,0:T(8,128)(2,1)S(1)} %get-tuple-element.26.both, f32[1072,128]{1,0:T(8,128)S(1)} %shard_map.87.aux, f32[1072,128]{1,0:T(8,128)S(1)} %collective-permute-done.2.aux_other, ...), custom_call_target="tpu_custom_call" | custom-call | flops 1073741824 | bytes 3588096 | tf_op jit(solution)/shard_map/pallas_call | solution.py:65
  62.9 1.9 %collective-permute-start.12 = (f32[128,256]{1,0:T(8,128)S(1)}, f32[128,256]{1,0:T(8,128)S(1)}, u32[]{:S(2)}, u32[]{:S(2)}) collective-permute-start(f32[128,256]{1,0:T(8,128)S(1)} %get-tuple-element.38), channel_id=1, source_target_pairs={{0,1},{1,0},{2,3},{3,2},{4,5},{5,4},{6,7},{7,6},{8,9},{9,8},{10,11... | collective-permute-start | bytes 393224 | tf_op jit(solution)/shard_map/ppermute | solution.py:33
  66.2 5.6 %collective-permute-start.13 = (f32[192,256]{1,0:T(8,128)S(1)}, f32[192,256]{1,0:T(8,128)S(1)}, u32[]{:S(2)}, u32[]{:S(2)}) collective-permute-start(f32[192,256]{1,0:T(8,128)S(1)} %get-tuple-element.41), channel_id=1, source_target_pairs={{0,2},{1,3},{2,0},{3,1},{4,6},{5,7},{6,4},{7,5},{8,10},{9,11},{10,... | collective-permute-start | bytes 589832 | tf_op jit(solution)/shard_map/ppermute | solution.py:33
  73.2 3.8 %collective-permute-done.13.came = f32[192,256]{1,0:T(8,128)S(1)} collective-permute-done((f32[192,256]{1,0:T(8,128)S(1)}, f32[192,256]{1,0:T(8,128)S(1)}, u32[]{:S(2)}, u32[]{:S(2)}) %collective-permute-start.13) | collective-permute-done | bytes 196640 | tf_op jit(solution)/shard_map/ppermute | solution.py:33
  77.1 2.8 %collective-permute-start.14 = (f32[96,256]{1,0:T(8,128)S(1)}, f32[96,256]{1,0:T(8,128)S(1)}, u32[]{:S(2)}, u32[]{:S(2)}) collective-permute-start(f32[96,256]{1,0:T(8,128)S(1)} %get-tuple-element.43), channel_id=1, source_target_pairs={{0,4},{1,5},{2,6},{3,7},{4,0},{5,1},{6,2},{7,3},{8,12},{9,13},{10,... | collective-permute-start | bytes 294920 | tf_op jit(solution)/shard_map/ppermute | solution.py:33
  79.9 4.2 %shard_map.89 = (f32[64,256]{1,0:T(8,128)S(1)}, f32[64,256]{1,0:T(8,128)S(1)}, bf16[16384,128]{1,0:T(8,128)(2,1)S(1)}) custom-call(bf16[16384,128]{1,0:T(8,128)(2,1)S(1)} %get-tuple-element.31.table, bf16[2048,1664]{1,0:T(8,128)(2,1)S(1)} %get-tuple-element.32.matrix, f32[2048,128]{1,0:T(8,128)S(1)} %get-tuple-element.33.start, ...), custom_call_target="tpu_custom_call", output_to_operand_aliasing={{2}: (0, {})} | custom-call | flops 1073741824 | bytes 17973248 | tf_op jit(solution)/shard_map/pallas_call | solution.py:65
  84.1 2.7 %collective-permute-start.10 = (f32[64,256]{1,0:T(8,128)S(1)}, f32[64,256]{1,0:T(8,128)S(1)}, u32[]{:S(2)}, u32[]{:S(2)}) collective-permute-start(f32[64,256]{1,0:T(8,128)S(1)} %get-tuple-element.36), channel_id=1, source_target_pairs={{0,2},{1,3},{2,0},{3,1},{4,6},{5,7},{6,4},{7,5},{8,10},{9,11},{10,... | collective-permute-start | bytes 196616 | tf_op jit(solution)/shard_map/ppermute | solution.py:33
  86.9 3.4 %collective-permute-done.10.came = f32[64,256]{1,0:T(8,128)S(1)} collective-permute-done((f32[64,256]{1,0:T(8,128)S(1)}, f32[64,256]{1,0:T(8,128)S(1)}, u32[]{:S(2)}, u32[]{:S(2)}) %collective-permute-start.10) | collective-permute-done | bytes 65568 | tf_op jit(solution)/shard_map/ppermute | solution.py:33
  90.3 7.7 %collective-permute-start.16 = (f32[80,256]{1,0:T(8,128)S(1)}, f32[80,256]{1,0:T(8,128)S(1)}, u32[]{:S(2)}, u32[]{:S(2)}) collective-permute-start(f32[80,256]{1,0:T(8,128)S(1)} %get-tuple-element.47), channel_id=1, source_target_pairs={{0,8},{1,9},{2,10},{3,11},{4,12},{5,13},{6,14},{7,15},{8,0},{9,1},... | collective-permute-start | bytes 245768 | tf_op jit(solution)/shard_map/ppermute | solution.py:33
  100.7 4.5 %collective-permute-done.15.one = f32[64,256]{1,0:T(8,128)S(1)} collective-permute-done((f32[64,256]{1,0:T(8,128)S(1)}, f32[64,256]{1,0:T(8,128)S(1)}, u32[]{:S(2)}, u32[]{:S(2)}) %collective-permute-start.15) | collective-permute-done | bytes 65568 | tf_op jit(solution)/shard_map/ppermute | solution.py:33
  105.1 2.9 %collective-permute-done.17.three = f32[64,256]{1,0:T(8,128)S(1)} collective-permute-done((f32[64,256]{1,0:T(8,128)S(1)}, f32[64,256]{1,0:T(8,128)S(1)}, u32[]{:S(2)}, u32[]{:S(2)}) %collective-permute-start.17) | collective-permute-done | bytes 65568 | tf_op jit(solution)/shard_map/ppermute | solution.py:33
  (37 shorter events, 14.7 us)
Async XLA Ops:
  0.6 71.2 %copy-start = (bf16[1,1024,1664]{2,1,0:T(8,128)(2,1)S(1)}, bf16[1,1024,1664]{2,1,0:T(8,128)(2,1)}, u32[]{:S(2)}) copy-start(bf16[1,1024,1664]{2,1,0:T(8,128)(2,1)} %refs_1_.1) | copy-start | bytes 10223620
  0.6 41.9 %collective-permute-start.1 = (bf16[1024,1664]{1,0:T(8,128)(2,1)}, bf16[1024,1664]{1,0:T(8,128)(2,1)S(1)}, u32[]{:S(2)}, u32[]{:S(2)}) collective-permute-start(bf16[1024,1664]{1,0:T(8,128)(2,1)} %bitcast.9), channel_id=1, source_target_pairs={{0,1},{1,0},{2,3},{3,2},{4,5},{5,4},{6,7},{7,6},{8,9},{9,8},{10,11... | collective-permute-start | bytes 10223624 | tf_op jit(solution)/shard_map/ppermute | solution.py:33
  2.8 7.0 %collective-permute-start = (bf16[1024,256]{1,0:T(8,128)(2,1)}, bf16[1024,256]{1,0:T(8,128)(2,1)S(1)}, u32[]{:S(2)}, u32[]{:S(2)}) collective-permute-start(bf16[1024,256]{1,0:T(8,128)(2,1)} %bitcast.10), channel_id=1, source_target_pairs={{0,1},{1,0},{2,3},{3,2},{4,5},{5,4},{6,7},{7,6},{8,9},{9,8},{10,11... | collective-permute-start | bytes 1572872 | tf_op jit(solution)/shard_map/ppermute | solution.py:33
  9.8 1.0 copy-start.1
  11.3 14.9 %collective-permute-start.3 = (bf16[2048,128]{1,0:T(8,128)(2,1)S(1)}, bf16[2048,128]{1,0:T(8,128)(2,1)S(1)}, u32[]{:S(2)}, u32[]{:S(2)}) collective-permute-start(bf16[2048,128]{1,0:T(8,128)(2,1)S(1)} %get-tuple-element.30.refs_3_), channel_id=1, source_target_pairs={{0,2},{1,15},{2,4},{3,1},{4,6},{5,3},{6,8},{7,5},{8,10},{9,7},{10,... | collective-permute-start | bytes 1572872 | tf_op jit(solution)/shard_map/ppermute | solution.py:33
  14.8 1.0 copy-start.2
  15.7 0.7 copy-start.3
  16.4 0.7 copy-start.5
  18.5 53.4 %copy-start.4 = (s32[1,16,26]{2,1,0:T(8,128)S(1)}, s32[1,16,26]{2,1,0:T(8,128)}, u32[]{:S(2)}) copy-start(s32[1,16,26]{2,1,0:T(8,128)} %refs_0_.1) | copy-start | bytes 4996
  18.6 14.8 %collective-permute-start.4 = (bf16[2048,128]{1,0:T(8,128)(2,1)S(1)}, bf16[2048,128]{1,0:T(8,128)(2,1)S(1)}, u32[]{:S(2)}, u32[]{:S(2)}) collective-permute-start(bf16[2048,128]{1,0:T(8,128)(2,1)S(1)} %get-tuple-element.30.refs_3_), channel_id=1, source_target_pairs={{0,14},{1,3},{2,0},{3,5},{4,2},{5,7},{6,4},{7,9},{8,6},{9,11},{10,... | collective-permute-start | bytes 1572872 | tf_op jit(solution)/shard_map/ppermute | solution.py:33
  26.2 14.4 %collective-permute-start.5 = (bf16[2048,128]{1,0:T(8,128)(2,1)S(1)}, bf16[2048,128]{1,0:T(8,128)(2,1)S(1)}, u32[]{:S(2)}, u32[]{:S(2)}) collective-permute-start(bf16[2048,128]{1,0:T(8,128)(2,1)S(1)} %collective-permute-done.3.refs_4_), channel_id=1, source_target_pairs={{0,2},{1,15},{2,4},{3,1},{4,6},{5,3},{6,8},{7,5},{8,10},{9,7},{10,... | collective-permute-start | bytes 1572872 | tf_op jit(solution)/shard_map/ppermute | solution.py:33
  28.1 31.9 %collective-permute-start.11 = (bf16[2048,256]{1,0:T(8,128)(2,1)S(1)}, bf16[2048,256]{1,0:T(8,128)(2,1)S(1)}, u32[]{:S(2)}, u32[]{:S(2)}) collective-permute-start(bf16[2048,256]{1,0:T(8,128)(2,1)S(1)} %get-tuple-element.26.both), channel_id=1, source_target_pairs={{0,16},{1,33},{2,18},{3,35},{4,20},{5,37},{6,22},{7,39},{8,24},{9,... | collective-permute-start | bytes 3145736 | tf_op jit(solution)/shard_map/ppermute | solution.py:33
  33.4 18.7 %collective-permute-start.6 = (bf16[2048,128]{1,0:T(8,128)(2,1)S(1)}, bf16[2048,128]{1,0:T(8,128)(2,1)S(1)}, u32[]{:S(2)}, u32[]{:S(2)}) collective-permute-start(bf16[2048,128]{1,0:T(8,128)(2,1)S(1)} %collective-permute-done.4.refs_5_), channel_id=1, source_target_pairs={{0,14},{1,3},{2,0},{3,5},{4,2},{5,7},{6,4},{7,9},{8,6},{9,11},{10,... | collective-permute-start | bytes 1572872 | tf_op jit(solution)/shard_map/ppermute | solution.py:33
  40.6 17.4 %collective-permute-start.7 = (bf16[2048,128]{1,0:T(8,128)(2,1)S(1)}, bf16[2048,128]{1,0:T(8,128)(2,1)S(1)}, u32[]{:S(2)}, u32[]{:S(2)}) collective-permute-start(bf16[2048,128]{1,0:T(8,128)(2,1)S(1)} %collective-permute-done.5.refs_6_), channel_id=1, source_target_pairs={{0,2},{1,15},{2,4},{3,1},{4,6},{5,3},{6,8},{7,5},{8,10},{9,7},{10,... | collective-permute-start | bytes 1572872 | tf_op jit(solution)/shard_map/ppermute | solution.py:33
  42.5 17.4 %collective-permute-start.2 = (f32[1072,128]{1,0:T(8,128)S(1)}, f32[1072,128]{1,0:T(8,128)S(1)}, u32[]{:S(2)}, u32[]{:S(2)}) collective-permute-start(f32[1072,128]{1,0:T(8,128)S(1)} %shard_map.87.aux), channel_id=1, source_target_pairs={{0,1},{1,0},{2,3},{3,2},{4,5},{5,4},{6,7},{7,6},{8,9},{9,8},{10,11... | collective-permute-start | bytes 1646600 | tf_op jit(solution)/shard_map/ppermute | solution.py:33
  52.1 19.8 %collective-permute-start.8 = (bf16[2048,128]{1,0:T(8,128)(2,1)S(1)}, bf16[2048,128]{1,0:T(8,128)(2,1)S(1)}, u32[]{:S(2)}, u32[]{:S(2)}) collective-permute-start(bf16[2048,128]{1,0:T(8,128)(2,1)S(1)} %collective-permute-done.6.refs_7_), channel_id=1, source_target_pairs={{0,14},{1,3},{2,0},{3,5},{4,2},{5,7},{6,4},{7,9},{8,6},{9,11},{10,... | collective-permute-start | bytes 1572872 | tf_op jit(solution)/shard_map/ppermute | solution.py:33
  58.0 21.9 %collective-permute-start.9 = (bf16[2048,128]{1,0:T(8,128)(2,1)S(1)}, bf16[2048,128]{1,0:T(8,128)(2,1)S(1)}, u32[]{:S(2)}, u32[]{:S(2)}) collective-permute-start(bf16[2048,128]{1,0:T(8,128)(2,1)S(1)} %collective-permute-done.7.refs_8_), channel_id=1, source_target_pairs={{0,2},{1,15},{2,4},{3,1},{4,6},{5,3},{6,8},{7,5},{8,10},{9,7},{10,... | collective-permute-start | bytes 1572872 | tf_op jit(solution)/shard_map/ppermute | solution.py:33
  62.9 3.2 %collective-permute-start.12 = (f32[128,256]{1,0:T(8,128)S(1)}, f32[128,256]{1,0:T(8,128)S(1)}, u32[]{:S(2)}, u32[]{:S(2)}) collective-permute-start(f32[128,256]{1,0:T(8,128)S(1)} %get-tuple-element.38), channel_id=1, source_target_pairs={{0,1},{1,0},{2,3},{3,2},{4,5},{5,4},{6,7},{7,6},{8,9},{9,8},{10,11... | collective-permute-start | bytes 393224 | tf_op jit(solution)/shard_map/ppermute | solution.py:33
  66.2 10.8 %collective-permute-start.13 = (f32[192,256]{1,0:T(8,128)S(1)}, f32[192,256]{1,0:T(8,128)S(1)}, u32[]{:S(2)}, u32[]{:S(2)}) collective-permute-start(f32[192,256]{1,0:T(8,128)S(1)} %get-tuple-element.41), channel_id=1, source_target_pairs={{0,2},{1,3},{2,0},{3,1},{4,6},{5,7},{6,4},{7,5},{8,10},{9,11},{10,... | collective-permute-start | bytes 589832 | tf_op jit(solution)/shard_map/ppermute | solution.py:33
  77.1 13.2 %collective-permute-start.14 = (f32[96,256]{1,0:T(8,128)S(1)}, f32[96,256]{1,0:T(8,128)S(1)}, u32[]{:S(2)}, u32[]{:S(2)}) collective-permute-start(f32[96,256]{1,0:T(8,128)S(1)} %get-tuple-element.43), channel_id=1, source_target_pairs={{0,4},{1,5},{2,6},{3,7},{4,0},{5,1},{6,2},{7,3},{8,12},{9,13},{10,... | collective-permute-start | bytes 294920 | tf_op jit(solution)/shard_map/ppermute | solution.py:33
  84.1 6.2 %collective-permute-start.10 = (f32[64,256]{1,0:T(8,128)S(1)}, f32[64,256]{1,0:T(8,128)S(1)}, u32[]{:S(2)}, u32[]{:S(2)}) collective-permute-start(f32[64,256]{1,0:T(8,128)S(1)} %get-tuple-element.36), channel_id=1, source_target_pairs={{0,2},{1,3},{2,0},{3,1},{4,6},{5,7},{6,4},{7,5},{8,10},{9,11},{10,... | collective-permute-start | bytes 196616 | tf_op jit(solution)/shard_map/ppermute | solution.py:33
  90.3 17.7 %collective-permute-start.16 = (f32[80,256]{1,0:T(8,128)S(1)}, f32[80,256]{1,0:T(8,128)S(1)}, u32[]{:S(2)}, u32[]{:S(2)}) collective-permute-start(f32[80,256]{1,0:T(8,128)S(1)} %get-tuple-element.47), channel_id=1, source_target_pairs={{0,8},{1,9},{2,10},{3,11},{4,12},{5,13},{6,14},{7,15},{8,0},{9,1},... | collective-permute-start | bytes 245768 | tf_op jit(solution)/shard_map/ppermute | solution.py:33
  98.1 7.1 %collective-permute-start.15 = (f32[64,256]{1,0:T(8,128)S(1)}, f32[64,256]{1,0:T(8,128)S(1)}, u32[]{:S(2)}, u32[]{:S(2)}) collective-permute-start(f32[64,256]{1,0:T(8,128)S(1)} %get-tuple-element.46), channel_id=1, source_target_pairs={{4,0},{5,1},{6,2},{7,3},{16,20},{17,21},{18,22},{19,23},{44,40},{4... | collective-permute-start | bytes 196616 | tf_op jit(solution)/shard_map/ppermute | solution.py:33
  99.4 8.7 %collective-permute-start.17 = (f32[64,256]{1,0:T(8,128)S(1)}, f32[64,256]{1,0:T(8,128)S(1)}, u32[]{:S(2)}, u32[]{:S(2)}) collective-permute-start(f32[64,256]{1,0:T(8,128)S(1)} %get-tuple-element.46), channel_id=1, source_target_pairs={{12,0},{13,1},{14,2},{15,3},{24,20},{25,21},{26,22},{27,23},{36,40... | collective-permute-start | bytes 196616 | tf_op jit(solution)/shard_map/ppermute | solution.py:33
  (2 other events, 1.4 us)

commit v2 on v1

--- a/solution.py
+++ b/solution.py
@@ -116,11 +116,20 @@
     out[LINKS : LINKS + 2, 0:16] = links[0].astype(F32)
 
 
-def half_kernel(own, other, out, both):
+def mine(core):
+    return mine_of(256, lambda n: 64 * core + n + jnp.where(n >= 64, 64, 0))
+
+
+def first_kernel(own, held, half):
     _, _, core = place()
-    pick = mine_of(256, lambda n: 64 * core + n + jnp.where(n >= 64, 64, 0))
-    out[pl.ds(pl.multiple_of(core * 1024, 1024), 1024), :] = dot(own[...], pick).astype(BF16)
-    out[pl.ds(pl.multiple_of((1 - core) * 1024, 1024), 1024), :] = dot(other[...], pick).astype(BF16)
+    held[...] = own[...]
+    half[...] = dot(own[...], mine(core)).astype(BF16)
+
+
+def half_kernel(own, own_half, other, out, both):
+    _, _, core = place()
+    out[pl.ds(pl.multiple_of(core * 1024, 1024), 1024), :] = own_half[...]
+    out[pl.ds(pl.multiple_of((1 - core) * 1024, 1024), 1024), :] = dot(other[...], mine(core)).astype(BF16)
     both[0:1024, :] = own[...]
     both[1024:2048, :] = other[...]
 
@@ -268,13 +277,19 @@
     own = basis[0]
     links = links.transpose(0, 2, 1)
     other = send(own, to_core)
-    half, both = call(half_kernel, [shape(2048, 128, dtype=BF16), shape(2048, 256, dtype=BF16)], [own, other])
+    own_held, own_half = call(first_kernel, [shape(1024, 256, dtype=BF16), shape(1024, 128, dtype=BF16)], [own])
+    half, both = call(
+        half_kernel,
+        [shape(2048, 128, dtype=BF16), shape(2048, 256, dtype=BF16)],
+        [own_held, own_half, other],
+        flops=4 * 10**10,
+    )
     left1 = send(half, ring(True))
     (aux,) = call(
         aux_kernel,
         [shape(AUX, 128)],
         [],
-        [couple, after(kcols, half), links, shift, mass],
+        [couple, after(kcols, own_held), links, shift, mass],
         [
             pltpu.VMEM((1, 1024, 128), BF16),
             pltpu.VMEM((1, 16, 26), jnp.int32),
@@ -283,14 +298,13 @@
             pltpu.VMEM((1, 1024), F32),
             pltpu.SemaphoreType.DMA((5,)),
         ],
-    )
-    right1 = send(after(half, aux), ring(False))
+        vmem=56,
+    )
+    right1 = send(half, ring(False))
     partner = send(both, lambda leaf, row: (leaf ^ (1 + row % 2), row))
     stiff_other = send(stiff[0], to_core)
     aux_other = send(after(aux, stiff_other), to_core)
     left2, right2 = send(left1, ring(True)), send(right1, ring(False))
-    left3, right3 = send(left2, ring(True)), send(right2, ring(False))
-    left4 = send(left3, ring(True))
     go, keep, mass_part = call(
         early_kernel,
         [shape(128, 256)] * 3,
@@ -309,8 +323,10 @@
     )
     came = send(go, to_core)
     go, keep = call(turn_kernel, [shape(192, 256)] * 2, [keep, came, mass_part])
+    left3, right3 = send(left2, ring(True)), send(after(right2, go), ring(False))
+    left4 = send(left3, ring(True))
     came = send(go, to_side)
-    go, early_keep = call(split_kernel, [shape(96, 256)] * 2, [keep, came])
+    go, early_keep = call(split_kernel, [shape(96, 256)] * 2, [keep, came], flops=5 * 10**9)
     early_came = send(go, to_group(1))
 
     table, matrix, start, spots = call(

time: 110 us -> 95.6 us (0.87)
  the two profiles are of different devices: /device:TPU:8 before, /device:TPU:6 now
where the time goes in v2:
time: 95.6 us; the launch traced here: 93.9 us
  starting transfers between devices  55.6 us (58%)
  waiting for transfers between devices  23.6 us (25%)
  Pallas kernels  11.8 us (12%)
  local copies, waits for them, and re-layouts  2.1 us (2%)
    ppermute x18, starting transfers between devices, send(): return lax.ppermute(value, ('leaf', 'rows'), pairs)  55.6 us
    ppermute x18, waiting for transfers between devices, send(): return lax.ppermute(value, ('leaf', 'rows'), pairs)  23.6 us
    pallas_call x10, Pallas kernels, call(): pl.pallas_call(body, out_shape=outs, in_specs=[VMEM] * len(arrays) + [HBM...  11.8 us
    unnamed x8, local copies, waits for them, and re-layouts  2.1 us
  transfers between devices with their start and end apart: 18, of which 8 were waited for; matrix products, arithmetic and copies ran while one was open for 0% of the time, Pallas kernels for 12%

profile of v2, /device:TPU:6, one launch (start us, length us, event | category | flops | bytes accessed | tf_op | source)
XLA Modules:
  0.0 93.9 jit_solution(18185921011278528154)
XLA Ops:
  0.6 1.9 %collective-permute-start = (bf16[1024,256]{1,0:T(8,128)(2,1)}, bf16[1024,256]{1,0:T(8,128)(2,1)S(1)}, u32[]{:S(2)}, u32[]{:S(2)}) collective-permute-start(bf16[1024,256]{1,0:T(8,128)(2,1)} %bitcast.10), channel_id=1, source_target_pairs={{0,1},{1,0},{2,3},{3,2},{4,5},{5,4},{6,7},{7,6},{8,9},{9,8},{10,11... | collective-permute-start | bytes 1572872 | tf_op jit(solution)/shard_map/ppermute | solution.py:33
  2.6 2.4 %collective-permute-start.1 = (bf16[1024,1664]{1,0:T(8,128)(2,1)}, bf16[1024,1664]{1,0:T(8,128)(2,1)S(1)}, u32[]{:S(2)}, u32[]{:S(2)}) collective-permute-start(bf16[1024,1664]{1,0:T(8,128)(2,1)} %bitcast.9), channel_id=1, source_target_pairs={{0,1},{1,0},{2,3},{3,2},{4,5},{5,4},{6,7},{7,6},{8,9},{9,8},{10,11... | collective-permute-start | bytes 10223624 | tf_op jit(solution)/shard_map/ppermute | solution.py:33
  6.7 3.5 %collective-permute-start.3 = (bf16[2048,128]{1,0:T(8,128)(2,1)S(1)}, bf16[2048,128]{1,0:T(8,128)(2,1)S(1)}, u32[]{:S(2)}, u32[]{:S(2)}) collective-permute-start(bf16[2048,128]{1,0:T(8,128)(2,1)S(1)} %get-tuple-element.33.refs_3_), channel_id=1, source_target_pairs={{0,2},{1,15},{2,4},{3,1},{4,6},{5,3},{6,8},{7,5},{8,10},{9,7},{10,... | collective-permute-start | bytes 1572872 | tf_op jit(solution)/shard_map/ppermute | solution.py:33
  10.2 4.3 %collective-permute-start.8 = (bf16[2048,256]{1,0:T(8,128)(2,1)S(1)}, bf16[2048,256]{1,0:T(8,128)(2,1)S(1)}, u32[]{:S(2)}, u32[]{:S(2)}) collective-permute-start(bf16[2048,256]{1,0:T(8,128)(2,1)S(1)} %get-tuple-element.30.both), channel_id=1, source_target_pairs={{0,16},{1,33},{2,18},{3,35},{4,20},{5,37},{6,22},{7,39},{8,24},{9,... | collective-permute-start | bytes 3145736 | tf_op jit(solution)/shard_map/ppermute | solution.py:33
  14.5 3.8 %collective-permute-start.4 = (bf16[2048,128]{1,0:T(8,128)(2,1)S(1)}, bf16[2048,128]{1,0:T(8,128)(2,1)S(1)}, u32[]{:S(2)}, u32[]{:S(2)}) collective-permute-start(bf16[2048,128]{1,0:T(8,128)(2,1)S(1)} %get-tuple-element.33.refs_3_), channel_id=1, source_target_pairs={{0,14},{1,3},{2,0},{3,5},{4,2},{5,7},{6,4},{7,9},{8,6},{9,11},{10,... | collective-permute-start | bytes 1572872 | tf_op jit(solution)/shard_map/ppermute | solution.py:33
  19.2 2.0 %collective-permute-start.5 = (bf16[2048,128]{1,0:T(8,128)(2,1)S(1)}, bf16[2048,128]{1,0:T(8,128)(2,1)S(1)}, u32[]{:S(2)}, u32[]{:S(2)}) collective-permute-start(bf16[2048,128]{1,0:T(8,128)(2,1)S(1)} %collective-permute-done.3.refs_4_), channel_id=1, source_target_pairs={{0,2},{1,15},{2,4},{3,1},{4,6},{5,3},{6,8},{7,5},{8,10},{9,7},{10,... | collective-permute-start | bytes 1572872 | tf_op jit(solution)/shard_map/ppermute | solution.py:33
  21.2 1.9 %shard_map.88.aux = f32[1072,128]{1,0:T(8,128)} custom-call(bf16[1,1024,128]{2,1,0:T(8,128)(2,1)} %couple_at.1, s32[1,16,26]{2,1,0:T(8,128)} %refs_0_.1, s32[1,2,16]{2,1,0:T(2,128)} %bitcast.12, f32[1,1024]{1,0:T(1,128)} %shift_at.1, f32[1,1024]{1,0:T(1,128)} %mass_at.1), custom_call_target="tpu_custom_call" | custom-call | bytes 820992 | tf_op jit(solution)/shard_map/pallas_call | solution.py:65
  23.1 4.8 %collective-permute-start.2 = (f32[1072,128]{1,0:T(8,128)}, f32[1072,128]{1,0:T(8,128)S(1)}, u32[]{:S(2)}, u32[]{:S(2)}) collective-permute-start(f32[1072,128]{1,0:T(8,128)} %shard_map.88.aux), channel_id=1, source_target_pairs={{0,1},{1,0},{2,3},{3,2},{4,5},{5,4},{6,7},{7,6},{8,9},{9,8},{10,11... | collective-permute-start | bytes 1646600 | tf_op jit(solution)/shard_map/ppermute | solution.py:33
  27.9 3.1 %collective-permute-start.6 = (bf16[2048,128]{1,0:T(8,128)(2,1)S(1)}, bf16[2048,128]{1,0:T(8,128)(2,1)S(1)}, u32[]{:S(2)}, u32[]{:S(2)}) collective-permute-start(bf16[2048,128]{1,0:T(8,128)(2,1)S(1)} %collective-permute-done.4.refs_5_), channel_id=1, source_target_pairs={{0,14},{1,3},{2,0},{3,5},{4,2},{5,7},{6,4},{7,9},{8,6},{9,11},{10,... | collective-permute-start | bytes 1572872 | tf_op jit(solution)/shard_map/ppermute | solution.py:33
  31.0 3.5 %collective-permute-done.5.refs_6_ = bf16[2048,128]{1,0:T(8,128)(2,1)S(1)} collective-permute-done((bf16[2048,128]{1,0:T(8,128)(2,1)S(1)}, bf16[2048,128]{1,0:T(8,128)(2,1)S(1)}, u32[]{:S(2)}, u32[]{:S(2)}) %collective-permute-start.5) | collective-permute-done | bytes 524320 | tf_op jit(solution)/shard_map/ppermute | solution.py:33
  34.5 1.9 %collective-permute-start.7 = (bf16[2048,128]{1,0:T(8,128)(2,1)S(1)}, bf16[2048,128]{1,0:T(8,128)(2,1)S(1)}, u32[]{:S(2)}, u32[]{:S(2)}) collective-permute-start(bf16[2048,128]{1,0:T(8,128)(2,1)S(1)} %collective-permute-done.5.refs_6_), channel_id=1, source_target_pairs={{0,2},{1,15},{2,4},{3,1},{4,6},{5,3},{6,8},{7,5},{8,10},{9,7},{10,... | collective-permute-start | bytes 1572872 | tf_op jit(solution)/shard_map/ppermute | solution.py:33
  38.5 2.9 %shard_map.89 = (f32[128,256]{1,0:T(8,128)S(1)}, f32[128,256]{1,0:T(8,128)S(1)}, f32[128,256]{1,0:T(8,128)S(1)}) custom-call(bf16[2048,256]{1,0:T(8,128)(2,1)S(1)} %get-tuple-element.30.both, f32[1072,128]{1,0:T(8,128)S(1)} %copy-done.1, f32[1072,128]{1,0:T(8,128)S(1)} %collective-permute-done.2.aux_other, bf16[2048,256]{1,0:T(8,128)(2,1)S(1)} %collective-permute-done.8.partner), custom_call_target="tpu_custom_call" | custom-call | flops 1073741824 | bytes 3588096 | tf_op jit(solution)/shard_map/pallas_call | solution.py:65
  41.4 3.7 %collective-permute-start.9 = (f32[128,256]{1,0:T(8,128)S(1)}, f32[128,256]{1,0:T(8,128)S(1)}, u32[]{:S(2)}, u32[]{:S(2)}) collective-permute-start(f32[128,256]{1,0:T(8,128)S(1)} %get-tuple-element.35), channel_id=1, source_target_pairs={{0,1},{1,0},{2,3},{3,2},{4,5},{5,4},{6,7},{7,6},{8,9},{9,8},{10,11... | collective-permute-start | bytes 393224 | tf_op jit(solution)/shard_map/ppermute | solution.py:33
  46.2 2.5 %collective-permute-start.13 = (f32[192,256]{1,0:T(8,128)S(1)}, f32[192,256]{1,0:T(8,128)S(1)}, u32[]{:S(2)}, u32[]{:S(2)}) collective-permute-start(f32[192,256]{1,0:T(8,128)S(1)} %get-tuple-element.37), channel_id=1, source_target_pairs={{0,2},{1,3},{2,0},{3,1},{4,6},{5,7},{6,4},{7,5},{8,10},{9,11},{10,... | collective-permute-start | bytes 589832 | tf_op jit(solution)/shard_map/ppermute | solution.py:33
  48.7 4.7 %collective-permute-start.10 = (bf16[2048,128]{1,0:T(8,128)(2,1)S(1)}, bf16[2048,128]{1,0:T(8,128)(2,1)S(1)}, u32[]{:S(2)}, u32[]{:S(2)}) collective-permute-start(bf16[2048,128]{1,0:T(8,128)(2,1)S(1)} %collective-permute-done.6.refs_7_), channel_id=1, source_target_pairs={{0,14},{1,3},{2,0},{3,5},{4,2},{5,7},{6,4},{7,9},{8,6},{9,11},{10,... | collective-permute-start | bytes 1572872 | tf_op jit(solution)/shard_map/ppermute | solution.py:33
  53.4 1.9 %collective-permute-start.11 = (bf16[2048,128]{1,0:T(8,128)(2,1)S(1)}, bf16[2048,128]{1,0:T(8,128)(2,1)S(1)}, u32[]{:S(2)}, u32[]{:S(2)}) collective-permute-start(bf16[2048,128]{1,0:T(8,128)(2,1)S(1)} %collective-permute-done.7.refs_8_), channel_id=1, source_target_pairs={{0,2},{1,15},{2,4},{3,1},{4,6},{5,3},{6,8},{7,5},{8,10},{9,7},{10,... | collective-permute-start | bytes 1572872 | tf_op jit(solution)/shard_map/ppermute | solution.py:33
  55.5 4.3 %collective-permute-start.14 = (f32[96,256]{1,0:T(8,128)S(1)}, f32[96,256]{1,0:T(8,128)S(1)}, u32[]{:S(2)}, u32[]{:S(2)}) collective-permute-start(f32[96,256]{1,0:T(8,128)S(1)} %get-tuple-element.47), channel_id=1, source_target_pairs={{0,4},{1,5},{2,6},{3,7},{4,0},{5,1},{6,2},{7,3},{8,12},{9,13},{10,... | collective-permute-start | bytes 294920 | tf_op jit(solution)/shard_map/ppermute | solution.py:33
  59.7 6.6 %collective-permute-done.10.refs_9_ = bf16[2048,128]{1,0:T(8,128)(2,1)S(1)} collective-permute-done((bf16[2048,128]{1,0:T(8,128)(2,1)S(1)}, bf16[2048,128]{1,0:T(8,128)(2,1)S(1)}, u32[]{:S(2)}, u32[]{:S(2)}) %collective-permute-start.10) | collective-permute-done | bytes 524320 | tf_op jit(solution)/shard_map/ppermute | solution.py:33
  66.4 1.4 %shard_map.91 = (bf16[16384,128]{1,0:T(8,128)(2,1)S(1)}, bf16[2048,1664]{1,0:T(8,128)(2,1)S(1)}, f32[2048,128]{1,0:T(8,128)S(1)}, s32[32,128]{1,0:T(8,128)S(1)}) custom-call(bf16[2048,256]{1,0:T(8,128)(2,1)S(1)} %get-tuple-element.30.both, f32[1072,128]{1,0:T(8,128)S(1)} %copy-done.1, f32[1072,128]{1,0:T(8,128)S(1)} %collective-permute-done.2.aux_other, ...), custom_call_target="tpu_custom_call" | custom-call | bytes 24708736 | tf_op jit(solution)/shard_map/pallas_call | solution.py:65
  67.7 4.2 %shard_map.92 = (f32[64,256]{1,0:T(8,128)S(1)}, f32[64,256]{1,0:T(8,128)S(1)}, bf16[16384,128]{1,0:T(8,128)(2,1)S(1)}) custom-call(bf16[16384,128]{1,0:T(8,128)(2,1)S(1)} %get-tuple-element.39.table, bf16[2048,1664]{1,0:T(8,128)(2,1)S(1)} %get-tuple-element.40.matrix, f32[2048,128]{1,0:T(8,128)S(1)} %get-tuple-element.41.start, ...), custom_call_target="tpu_custom_call", output_to_operand_aliasing={{2}: (0, {})} | custom-call | flops 1073741824 | bytes 17973248 | tf_op jit(solution)/shard_map/pallas_call | solution.py:65
  72.0 2.6 %collective-permute-start.12 = (f32[64,256]{1,0:T(8,128)S(1)}, f32[64,256]{1,0:T(8,128)S(1)}, u32[]{:S(2)}, u32[]{:S(2)}) collective-permute-start(f32[64,256]{1,0:T(8,128)S(1)} %get-tuple-element.44), channel_id=1, source_target_pairs={{0,2},{1,3},{2,0},{3,1},{4,6},{5,7},{6,4},{7,5},{8,10},{9,11},{10,... | collective-permute-start | bytes 196616 | tf_op jit(solution)/shard_map/ppermute | solution.py:33
  74.6 3.5 %collective-permute-done.12.came = f32[64,256]{1,0:T(8,128)S(1)} collective-permute-done((f32[64,256]{1,0:T(8,128)S(1)}, f32[64,256]{1,0:T(8,128)S(1)}, u32[]{:S(2)}, u32[]{:S(2)}) %collective-permute-start.12) | collective-permute-done | bytes 65568 | tf_op jit(solution)/shard_map/ppermute | solution.py:33
  78.2 5.6 %collective-permute-start.16 = (f32[80,256]{1,0:T(8,128)S(1)}, f32[80,256]{1,0:T(8,128)S(1)}, u32[]{:S(2)}, u32[]{:S(2)}) collective-permute-start(f32[80,256]{1,0:T(8,128)S(1)} %get-tuple-element.51), channel_id=1, source_target_pairs={{0,8},{1,9},{2,10},{3,11},{4,12},{5,13},{6,14},{7,15},{8,0},{9,1},... | collective-permute-start | bytes 245768 | tf_op jit(solution)/shard_map/ppermute | solution.py:33
  86.3 6.0 %collective-permute-done.15.one = f32[64,256]{1,0:T(8,128)S(1)} collective-permute-done((f32[64,256]{1,0:T(8,128)S(1)}, f32[64,256]{1,0:T(8,128)S(1)}, u32[]{:S(2)}, u32[]{:S(2)}) %collective-permute-start.15) | collective-permute-done | bytes 65568 | tf_op jit(solution)/shard_map/ppermute | solution.py:33
  (30 shorter events, 9.9 us)
Async XLA Ops:
  0.6 5.7 %collective-permute-start = (bf16[1024,256]{1,0:T(8,128)(2,1)}, bf16[1024,256]{1,0:T(8,128)(2,1)S(1)}, u32[]{:S(2)}, u32[]{:S(2)}) collective-permute-start(bf16[1024,256]{1,0:T(8,128)(2,1)} %bitcast.10), channel_id=1, source_target_pairs={{0,1},{1,0},{2,3},{3,2},{4,5},{5,4},{6,7},{7,6},{8,9},{9,8},{10,11... | collective-permute-start | bytes 1572872 | tf_op jit(solution)/shard_map/ppermute | solution.py:33
  2.6 20.5 %collective-permute-start.1 = (bf16[1024,1664]{1,0:T(8,128)(2,1)}, bf16[1024,1664]{1,0:T(8,128)(2,1)S(1)}, u32[]{:S(2)}, u32[]{:S(2)}) collective-permute-start(bf16[1024,1664]{1,0:T(8,128)(2,1)} %bitcast.9), channel_id=1, source_target_pairs={{0,1},{1,0},{2,3},{3,2},{4,5},{5,4},{6,7},{7,6},{8,9},{9,8},{10,11... | collective-permute-start | bytes 10223624 | tf_op jit(solution)/shard_map/ppermute | solution.py:33
  5.0 1.0 %copy-start.2 = (bf16[1,1024,256]{2,1,0:T(8,128)(2,1)S(1)}, bf16[1,1024,256]{2,1,0:T(8,128)(2,1)}, u32[]{:S(2)}) copy-start(bf16[1,1024,256]{2,1,0:T(8,128)(2,1)} %param.7) | copy-start | bytes 1572868
  6.7 12.5 %collective-permute-start.3 = (bf16[2048,128]{1,0:T(8,128)(2,1)S(1)}, bf16[2048,128]{1,0:T(8,128)(2,1)S(1)}, u32[]{:S(2)}, u32[]{:S(2)}) collective-permute-start(bf16[2048,128]{1,0:T(8,128)(2,1)S(1)} %get-tuple-element.33.refs_3_), channel_id=1, source_target_pairs={{0,2},{1,15},{2,4},{3,1},{4,6},{5,3},{6,8},{7,5},{8,10},{9,7},{10,... | collective-permute-start | bytes 1572872 | tf_op jit(solution)/shard_map/ppermute | solution.py:33
  10.2 27.3 %collective-permute-start.8 = (bf16[2048,256]{1,0:T(8,128)(2,1)S(1)}, bf16[2048,256]{1,0:T(8,128)(2,1)S(1)}, u32[]{:S(2)}, u32[]{:S(2)}) collective-permute-start(bf16[2048,256]{1,0:T(8,128)(2,1)S(1)} %get-tuple-element.30.both), channel_id=1, source_target_pairs={{0,16},{1,33},{2,18},{3,35},{4,20},{5,37},{6,22},{7,39},{8,24},{9,... | collective-permute-start | bytes 3145736 | tf_op jit(solution)/shard_map/ppermute | solution.py:33
  14.5 13.5 %collective-permute-start.4 = (bf16[2048,128]{1,0:T(8,128)(2,1)S(1)}, bf16[2048,128]{1,0:T(8,128)(2,1)S(1)}, u32[]{:S(2)}, u32[]{:S(2)}) collective-permute-start(bf16[2048,128]{1,0:T(8,128)(2,1)S(1)} %get-tuple-element.33.refs_3_), channel_id=1, source_target_pairs={{0,14},{1,3},{2,0},{3,5},{4,2},{5,7},{6,4},{7,9},{8,6},{9,11},{10,... | collective-permute-start | bytes 1572872 | tf_op jit(solution)/shard_map/ppermute | solution.py:33
  19.2 15.3 %collective-permute-start.5 = (bf16[2048,128]{1,0:T(8,128)(2,1)S(1)}, bf16[2048,128]{1,0:T(8,128)(2,1)S(1)}, u32[]{:S(2)}, u32[]{:S(2)}) collective-permute-start(bf16[2048,128]{1,0:T(8,128)(2,1)S(1)} %collective-permute-done.3.refs_4_), channel_id=1, source_target_pairs={{0,2},{1,15},{2,4},{3,1},{4,6},{5,3},{6,8},{7,5},{8,10},{9,7},{10,... | collective-permute-start | bytes 1572872 | tf_op jit(solution)/shard_map/ppermute | solution.py:33
  23.1 14.3 %collective-permute-start.2 = (f32[1072,128]{1,0:T(8,128)}, f32[1072,128]{1,0:T(8,128)S(1)}, u32[]{:S(2)}, u32[]{:S(2)}) collective-permute-start(f32[1072,128]{1,0:T(8,128)} %shard_map.88.aux), channel_id=1, source_target_pairs={{0,1},{1,0},{2,3},{3,2},{4,5},{5,4},{6,7},{7,6},{8,9},{9,8},{10,11... | collective-permute-start | bytes 1646600 | tf_op jit(solution)/shard_map/ppermute | solution.py:33
  27.9 20.8 %collective-permute-start.6 = (bf16[2048,128]{1,0:T(8,128)(2,1)S(1)}, bf16[2048,128]{1,0:T(8,128)(2,1)S(1)}, u32[]{:S(2)}, u32[]{:S(2)}) collective-permute-start(bf16[2048,128]{1,0:T(8,128)(2,1)S(1)} %collective-permute-done.4.refs_5_), channel_id=1, source_target_pairs={{0,14},{1,3},{2,0},{3,5},{4,2},{5,7},{6,4},{7,9},{8,6},{9,11},{10,... | collective-permute-start | bytes 1572872 | tf_op jit(solution)/shard_map/ppermute | solution.py:33
  34.5 18.9 %collective-permute-start.7 = (bf16[2048,128]{1,0:T(8,128)(2,1)S(1)}, bf16[2048,128]{1,0:T(8,128)(2,1)S(1)}, u32[]{:S(2)}, u32[]{:S(2)}) collective-permute-start(bf16[2048,128]{1,0:T(8,128)(2,1)S(1)} %collective-permute-done.5.refs_6_), channel_id=1, source_target_pairs={{0,2},{1,15},{2,4},{3,1},{4,6},{5,3},{6,8},{7,5},{8,10},{9,7},{10,... | collective-permute-start | bytes 1572872 | tf_op jit(solution)/shard_map/ppermute | solution.py:33
  37.4 1.1 %copy-start.1 = (f32[1072,128]{1,0:T(8,128)S(1)}, f32[1072,128]{1,0:T(8,128)}, u32[]{:S(2)}) copy-start(f32[1072,128]{1,0:T(8,128)} %shard_map.88.aux) | copy-start | bytes 1646596
  41.4 4.7 %collective-permute-start.9 = (f32[128,256]{1,0:T(8,128)S(1)}, f32[128,256]{1,0:T(8,128)S(1)}, u32[]{:S(2)}, u32[]{:S(2)}) collective-permute-start(f32[128,256]{1,0:T(8,128)S(1)} %get-tuple-element.35), channel_id=1, source_target_pairs={{0,1},{1,0},{2,3},{3,2},{4,5},{5,4},{6,7},{7,6},{8,9},{9,8},{10,11... | collective-permute-start | bytes 393224 | tf_op jit(solution)/shard_map/ppermute | solution.py:33
  46.2 9.2 %collective-permute-start.13 = (f32[192,256]{1,0:T(8,128)S(1)}, f32[192,256]{1,0:T(8,128)S(1)}, u32[]{:S(2)}, u32[]{:S(2)}) collective-permute-start(f32[192,256]{1,0:T(8,128)S(1)} %get-tuple-element.37), channel_id=1, source_target_pairs={{0,2},{1,3},{2,0},{3,1},{4,6},{5,7},{6,4},{7,5},{8,10},{9,11},{10,... | collective-permute-start | bytes 589832 | tf_op jit(solution)/shard_map/ppermute | solution.py:33
  48.7 17.6 %collective-permute-start.10 = (bf16[2048,128]{1,0:T(8,128)(2,1)S(1)}, bf16[2048,128]{1,0:T(8,128)(2,1)S(1)}, u32[]{:S(2)}, u32[]{:S(2)}) collective-permute-start(bf16[2048,128]{1,0:T(8,128)(2,1)S(1)} %collective-permute-done.6.refs_7_), channel_id=1, source_target_pairs={{0,14},{1,3},{2,0},{3,5},{4,2},{5,7},{6,4},{7,9},{8,6},{9,11},{10,... | collective-permute-start | bytes 1572872 | tf_op jit(solution)/shard_map/ppermute | solution.py:33
  53.4 14.3 %collective-permute-start.11 = (bf16[2048,128]{1,0:T(8,128)(2,1)S(1)}, bf16[2048,128]{1,0:T(8,128)(2,1)S(1)}, u32[]{:S(2)}, u32[]{:S(2)}) collective-permute-start(bf16[2048,128]{1,0:T(8,128)(2,1)S(1)} %collective-permute-done.7.refs_8_), channel_id=1, source_target_pairs={{0,2},{1,15},{2,4},{3,1},{4,6},{5,3},{6,8},{7,5},{8,10},{9,7},{10,... | collective-permute-start | bytes 1572872 | tf_op jit(solution)/shard_map/ppermute | solution.py:33
  55.4 11.0 %copy-start = (bf16[1,1024,1664]{2,1,0:T(8,128)(2,1)S(1)}, bf16[1,1024,1664]{2,1,0:T(8,128)(2,1)}, u32[]{:S(2)}) copy-start(bf16[1,1024,1664]{2,1,0:T(8,128)(2,1)} %refs_1_.1) | copy-start | bytes 10223620
  55.4 11.0 %copy-start.3 = (s32[1,16,26]{2,1,0:T(8,128)S(1)}, s32[1,16,26]{2,1,0:T(8,128)}, u32[]{:S(2)}) copy-start(s32[1,16,26]{2,1,0:T(8,128)} %refs_0_.1) | copy-start | bytes 4996
  55.5 19.1 %collective-permute-start.14 = (f32[96,256]{1,0:T(8,128)S(1)}, f32[96,256]{1,0:T(8,128)S(1)}, u32[]{:S(2)}, u32[]{:S(2)}) collective-permute-start(f32[96,256]{1,0:T(8,128)S(1)} %get-tuple-element.47), channel_id=1, source_target_pairs={{0,4},{1,5},{2,6},{3,7},{4,0},{5,1},{6,2},{7,3},{8,12},{9,13},{10,... | collective-permute-start | bytes 294920 | tf_op jit(solution)/shard_map/ppermute | solution.py:33
  72.0 6.2 %collective-permute-start.12 = (f32[64,256]{1,0:T(8,128)S(1)}, f32[64,256]{1,0:T(8,128)S(1)}, u32[]{:S(2)}, u32[]{:S(2)}) collective-permute-start(f32[64,256]{1,0:T(8,128)S(1)} %get-tuple-element.44), channel_id=1, source_target_pairs={{0,2},{1,3},{2,0},{3,1},{4,6},{5,7},{6,4},{7,5},{8,10},{9,11},{10,... | collective-permute-start | bytes 196616 | tf_op jit(solution)/shard_map/ppermute | solution.py:33
  78.2 15.1 %collective-permute-start.16 = (f32[80,256]{1,0:T(8,128)S(1)}, f32[80,256]{1,0:T(8,128)S(1)}, u32[]{:S(2)}, u32[]{:S(2)}) collective-permute-start(f32[80,256]{1,0:T(8,128)S(1)} %get-tuple-element.51), channel_id=1, source_target_pairs={{0,8},{1,9},{2,10},{3,11},{4,12},{5,13},{6,14},{7,15},{8,0},{9,1},... | collective-permute-start | bytes 245768 | tf_op jit(solution)/shard_map/ppermute | solution.py:33
  83.7 8.6 %collective-permute-start.15 = (f32[64,256]{1,0:T(8,128)S(1)}, f32[64,256]{1,0:T(8,128)S(1)}, u32[]{:S(2)}, u32[]{:S(2)}) collective-permute-start(f32[64,256]{1,0:T(8,128)S(1)} %get-tuple-element.50), channel_id=1, source_target_pairs={{4,0},{5,1},{6,2},{7,3},{16,20},{17,21},{18,22},{19,23},{44,40},{4... | collective-permute-start | bytes 196616 | tf_op jit(solution)/shard_map/ppermute | solution.py:33
  85.0 8.3 %collective-permute-start.17 = (f32[64,256]{1,0:T(8,128)S(1)}, f32[64,256]{1,0:T(8,128)S(1)}, u32[]{:S(2)}, u32[]{:S(2)}) collective-permute-start(f32[64,256]{1,0:T(8,128)S(1)} %get-tuple-element.50), channel_id=1, source_target_pairs={{12,0},{13,1},{14,2},{15,3},{24,20},{25,21},{26,22},{27,23},{36,40... | collective-permute-start | bytes 196616 | tf_op jit(solution)/shard_map/ppermute | solution.py:33

commit v3 on v2

--- a/solution.py
+++ b/solution.py
@@ -143,7 +143,15 @@
             )
 
 
-def early_kernel(both, aux, aux_other, partner, to_send, to_keep, mred, coupled, weights, masked, spots, at, sem):
+def mass_kernel(both, aux, aux_other, mred, weights):
+    _, _, core = place()
+    spread(weights, aux[MASS : MASS + 8, :], aux_other[MASS : MASS + 8, :])
+    pick = mine_of(256, lambda n: 64 * ((n % 64) // 16) + 32 * (n // 64) + 16 * core + n % 16)
+    weighted = (weights[...] * dot(both[...], pick)).astype(BF16)
+    mred[...] = dot_t(weighted, both[...])
+
+
+def early_kernel(both, aux, aux_other, partner, to_send, to_keep, coupled, masked, spots, at, sem):
     _, _, core = place()
     spots[...] = jnp.zeros((8, 128), jnp.int32)
     for part, rows in enumerate((aux, aux_other)):
@@ -163,11 +171,7 @@
         coupled[rows, :] = dot(masked[rows, :], jnp.concatenate([block, block], axis=0)).astype(BF16)
         return carry
 
-    lax.fori_loop(0, 32, one, 0, unroll=8)
-    spread(weights, aux[MASS : MASS + 8, :], aux_other[MASS : MASS + 8, :])
-    pick = mine_of(256, lambda n: 64 * ((n % 64) // 16) + 32 * (n // 64) + 16 * core + n % 16)
-    weighted = (weights[...] * dot(both[...], pick)).astype(BF16)
-    mred[...] = dot_t(weighted, both[...])
+    lax.fori_loop(0, 32, one, 0, unroll=16)
     term = dot_t(coupled[...], both[...])
     for k in range(2):
         low, high = term[k * 128 : k * 128 + 64, :], term[k * 128 + 64 : k * 128 + 128, :]
@@ -245,7 +249,7 @@
         image[rows, :] = total.astype(BF16)
         return carry
 
-    lax.fori_loop(0, 32, one, 0, unroll=8)
+    lax.fori_loop(0, 32, one, 0, unroll=16)
     result = dot_t(image[...], both[...])
     low, high = result[0:64, :], result[64:128, :]
     to_send[...] = jnp.where(side == 0, high, low)
@@ -304,15 +308,17 @@
     partner = send(both, lambda leaf, row: (leaf ^ (1 + row % 2), row))
     stiff_other = send(stiff[0], to_core)
     aux_other = send(after(aux, stiff_other), to_core)
+    (mass_part,) = call(
+        mass_kernel, [shape(128, 256)], [both, aux, aux_other], [], [pltpu.VMEM((2048, 128), F32)], 0
+    )
     left2, right2 = send(left1, ring(True)), send(right1, ring(False))
-    go, keep, mass_part = call(
+    go, keep = call(
         early_kernel,
-        [shape(128, 256)] * 3,
+        [shape(128, 256)] * 2,
         [both, aux, aux_other, partner],
         [],
         [
             pltpu.VMEM((2048, 256), BF16),
-            pltpu.VMEM((2048, 128), F32),
             pltpu.VMEM((2048, 128), BF16),
             pltpu.VMEM((8, 128), jnp.int32),
             pltpu.SMEM((8, 128), jnp.int32),

time: 95.6 us -> 94.2 us (0.985)
  waiting for transfers between devices: 23.6 us -> 22.3 us
    ppermute x18, waiting for transfers between devices: 23.6 us -> 22.3 us  [send(): return lax.ppermute(value, ('leaf', 'rows'), pairs)]
    pallas_call x10 -> x11, Pallas kernels: 11.8 us -> 11.3 us  [call(): pl.pallas_call(body, out_shape=outs, in_specs=[VMEM] * len(arrays) + [HBM...]
    unnamed x8 -> x10, local copies, waits for them, and re-layouts: 2.1 us -> 2.1 us
  transfers between devices with their start and end apart: 18 -> 18, of which waited for: 8 -> 7; matrix products, arithmetic and copies ran while one was open for 0% -> 0% of each run, Pallas kernels for 12% -> 11%
where the time goes in v3:
time: 94.2 us; the launch traced here: 92.5 us
  starting transfers between devices  55.9 us (59%)
  waiting for transfers between devices  22.3 us (24%)
  Pallas kernels  11.3 us (12%)
  local copies, waits for them, and re-layouts  2.1 us (2%)
  between operations  0.96 us (1%)
    ppermute x18, starting transfers between devices, send(): return lax.ppermute(value, ('leaf', 'rows'), pairs)  55.9 us
    ppermute x18, waiting for transfers between devices, send(): return lax.ppermute(value, ('leaf', 'rows'), pairs)  22.3 us
    pallas_call x11, Pallas kernels, call(): pl.pallas_call(body, out_shape=outs, in_specs=[VMEM] * len(arrays) + [HBM...  11.3 us
    unnamed x10, local copies, waits for them, and re-layouts  2.1 us
  transfers between devices with their start and end apart: 18, of which 7 were waited for; matrix products, arithmetic and copies ran while one was open for 0% of the time, Pallas kernels for 11%

profile of v3, /device:TPU:6, one launch (start us, length us, event | category | flops | bytes accessed | tf_op | source)
XLA Modules:
  0.0 92.5 jit_solution(12335120283270944463)
XLA Ops:
  0.6 1.9 %collective-permute-start = (bf16[1024,256]{1,0:T(8,128)(2,1)}, bf16[1024,256]{1,0:T(8,128)(2,1)S(1)}, u32[]{:S(2)}, u32[]{:S(2)}) collective-permute-start(bf16[1024,256]{1,0:T(8,128)(2,1)} %bitcast.10), channel_id=1, source_target_pairs={{0,1},{1,0},{2,3},{3,2},{4,5},{5,4},{6,7},{7,6},{8,9},{9,8},{10,11... | collective-permute-start | bytes 1572872 | tf_op jit(solution)/shard_map/ppermute | solution.py:33
  2.6 2.4 %collective-permute-start.1 = (bf16[1024,1664]{1,0:T(8,128)(2,1)}, bf16[1024,1664]{1,0:T(8,128)(2,1)S(1)}, u32[]{:S(2)}, u32[]{:S(2)}) collective-permute-start(bf16[1024,1664]{1,0:T(8,128)(2,1)} %bitcast.9), channel_id=1, source_target_pairs={{0,1},{1,0},{2,3},{3,2},{4,5},{5,4},{6,7},{7,6},{8,9},{9,8},{10,11... | collective-permute-start | bytes 10223624 | tf_op jit(solution)/shard_map/ppermute | solution.py:33
  6.7 3.5 %collective-permute-start.3 = (bf16[2048,128]{1,0:T(8,128)(2,1)S(1)}, bf16[2048,128]{1,0:T(8,128)(2,1)S(1)}, u32[]{:S(2)}, u32[]{:S(2)}) collective-permute-start(bf16[2048,128]{1,0:T(8,128)(2,1)S(1)} %get-tuple-element.32.refs_3_), channel_id=1, source_target_pairs={{0,2},{1,15},{2,4},{3,1},{4,6},{5,3},{6,8},{7,5},{8,10},{9,7},{10,... | collective-permute-start | bytes 1572872 | tf_op jit(solution)/shard_map/ppermute | solution.py:33
  10.2 4.3 %collective-permute-start.8 = (bf16[2048,256]{1,0:T(8,128)(2,1)S(1)}, bf16[2048,256]{1,0:T(8,128)(2,1)S(1)}, u32[]{:S(2)}, u32[]{:S(2)}) collective-permute-start(bf16[2048,256]{1,0:T(8,128)(2,1)S(1)} %get-tuple-element.29.both), channel_id=1, source_target_pairs={{0,16},{1,33},{2,18},{3,35},{4,20},{5,37},{6,22},{7,39},{8,24},{9,... | collective-permute-start | bytes 3145736 | tf_op jit(solution)/shard_map/ppermute | solution.py:33
  14.5 3.8 %collective-permute-start.4 = (bf16[2048,128]{1,0:T(8,128)(2,1)S(1)}, bf16[2048,128]{1,0:T(8,128)(2,1)S(1)}, u32[]{:S(2)}, u32[]{:S(2)}) collective-permute-start(bf16[2048,128]{1,0:T(8,128)(2,1)S(1)} %get-tuple-element.32.refs_3_), channel_id=1, source_target_pairs={{0,14},{1,3},{2,0},{3,5},{4,2},{5,7},{6,4},{7,9},{8,6},{9,11},{10,... | collective-permute-start | bytes 1572872 | tf_op jit(solution)/shard_map/ppermute | solution.py:33
  19.2 2.0 %collective-permute-start.5 = (bf16[2048,128]{1,0:T(8,128)(2,1)S(1)}, bf16[2048,128]{1,0:T(8,128)(2,1)S(1)}, u32[]{:S(2)}, u32[]{:S(2)}) collective-permute-start(bf16[2048,128]{1,0:T(8,128)(2,1)S(1)} %collective-permute-done.3.refs_4_), channel_id=1, source_target_pairs={{0,2},{1,15},{2,4},{3,1},{4,6},{5,3},{6,8},{7,5},{8,10},{9,7},{10,... | collective-permute-start | bytes 1572872 | tf_op jit(solution)/shard_map/ppermute | solution.py:33
  21.2 1.9 %shard_map.88.aux = f32[1072,128]{1,0:T(8,128)} custom-call(bf16[1,1024,128]{2,1,0:T(8,128)(2,1)} %couple_at.1, s32[1,16,26]{2,1,0:T(8,128)} %refs_0_.1, s32[1,2,16]{2,1,0:T(2,128)} %bitcast.12, f32[1,1024]{1,0:T(1,128)} %shift_at.1, f32[1,1024]{1,0:T(1,128)} %mass_at.1), custom_call_target="tpu_custom_call" | custom-call | bytes 820992 | tf_op jit(solution)/shard_map/pallas_call | solution.py:65
  23.1 4.8 %collective-permute-start.2 = (f32[1072,128]{1,0:T(8,128)}, f32[1072,128]{1,0:T(8,128)S(1)}, u32[]{:S(2)}, u32[]{:S(2)}) collective-permute-start(f32[1072,128]{1,0:T(8,128)} %shard_map.88.aux), channel_id=1, source_target_pairs={{0,1},{1,0},{2,3},{3,2},{4,5},{5,4},{6,7},{7,6},{8,9},{9,8},{10,11... | collective-permute-start | bytes 1646600 | tf_op jit(solution)/shard_map/ppermute | solution.py:33
  27.9 3.1 %collective-permute-start.6 = (bf16[2048,128]{1,0:T(8,128)(2,1)S(1)}, bf16[2048,128]{1,0:T(8,128)(2,1)S(1)}, u32[]{:S(2)}, u32[]{:S(2)}) collective-permute-start(bf16[2048,128]{1,0:T(8,128)(2,1)S(1)} %collective-permute-done.4.refs_5_), channel_id=1, source_target_pairs={{0,14},{1,3},{2,0},{3,5},{4,2},{5,7},{6,4},{7,9},{8,6},{9,11},{10,... | collective-permute-start | bytes 1572872 | tf_op jit(solution)/shard_map/ppermute | solution.py:33
  31.0 3.5 %collective-permute-done.5.refs_6_ = bf16[2048,128]{1,0:T(8,128)(2,1)S(1)} collective-permute-done((bf16[2048,128]{1,0:T(8,128)(2,1)S(1)}, bf16[2048,128]{1,0:T(8,128)(2,1)S(1)}, u32[]{:S(2)}, u32[]{:S(2)}) %collective-permute-start.5) | collective-permute-done | bytes 524320 | tf_op jit(solution)/shard_map/ppermute | solution.py:33
  34.5 1.9 %collective-permute-start.7 = (bf16[2048,128]{1,0:T(8,128)(2,1)S(1)}, bf16[2048,128]{1,0:T(8,128)(2,1)S(1)}, u32[]{:S(2)}, u32[]{:S(2)}) collective-permute-start(bf16[2048,128]{1,0:T(8,128)(2,1)S(1)} %collective-permute-done.5.refs_6_), channel_id=1, source_target_pairs={{0,2},{1,15},{2,4},{3,1},{4,6},{5,3},{6,8},{7,5},{8,10},{9,7},{10,... | collective-permute-start | bytes 1572872 | tf_op jit(solution)/shard_map/ppermute | solution.py:33
  38.5 1.8 %shard_map.89 = (f32[128,256]{1,0:T(8,128)S(1)}, f32[128,256]{1,0:T(8,128)S(1)}) custom-call(bf16[2048,256]{1,0:T(8,128)(2,1)S(1)} %get-tuple-element.29.both, f32[1072,128]{1,0:T(8,128)S(1)} %copy-done, f32[1072,128]{1,0:T(8,128)S(1)} %collective-permute-done.2.aux_other, bf16[2048,256]{1,0:T(8,128)(2,1)S(1)} %collective-permute-done.8.partner), custom_call_target="tpu_custom_call" | custom-call | flops 1073741824 | bytes 3457024 | tf_op jit(solution)/shard_map/pallas_call | solution.py:65
  40.3 3.7 %collective-permute-start.9 = (f32[128,256]{1,0:T(8,128)S(1)}, f32[128,256]{1,0:T(8,128)S(1)}, u32[]{:S(2)}, u32[]{:S(2)}) collective-permute-start(f32[128,256]{1,0:T(8,128)S(1)} %get-tuple-element.34), channel_id=1, source_target_pairs={{0,1},{1,0},{2,3},{3,2},{4,5},{5,4},{6,7},{7,6},{8,9},{9,8},{10,11... | collective-permute-start | bytes 393224 | tf_op jit(solution)/shard_map/ppermute | solution.py:33
  45.2 2.4 %collective-permute-start.13 = (f32[192,256]{1,0:T(8,128)S(1)}, f32[192,256]{1,0:T(8,128)S(1)}, u32[]{:S(2)}, u32[]{:S(2)}) collective-permute-start(f32[192,256]{1,0:T(8,128)S(1)} %get-tuple-element.35), channel_id=1, source_target_pairs={{0,2},{1,3},{2,0},{3,1},{4,6},{5,7},{6,4},{7,5},{8,10},{9,11},{10,... | collective-permute-start | bytes 589832 | tf_op jit(solution)/shard_map/ppermute | solution.py:33
  47.6 4.7 %collective-permute-start.10 = (bf16[2048,128]{1,0:T(8,128)(2,1)S(1)}, bf16[2048,128]{1,0:T(8,128)(2,1)S(1)}, u32[]{:S(2)}, u32[]{:S(2)}) collective-permute-start(bf16[2048,128]{1,0:T(8,128)(2,1)S(1)} %collective-permute-done.6.refs_7_), channel_id=1, source_target_pairs={{0,14},{1,3},{2,0},{3,5},{4,2},{5,7},{6,4},{7,9},{8,6},{9,11},{10,... | collective-permute-start | bytes 1572872 | tf_op jit(solution)/shard_map/ppermute | solution.py:33
  52.3 1.9 %collective-permute-start.11 = (bf16[2048,128]{1,0:T(8,128)(2,1)S(1)}, bf16[2048,128]{1,0:T(8,128)(2,1)S(1)}, u32[]{:S(2)}, u32[]{:S(2)}) collective-permute-start(bf16[2048,128]{1,0:T(8,128)(2,1)S(1)} %collective-permute-done.7.refs_8_), channel_id=1, source_target_pairs={{0,2},{1,15},{2,4},{3,1},{4,6},{5,3},{6,8},{7,5},{8,10},{9,7},{10,... | collective-permute-start | bytes 1572872 | tf_op jit(solution)/shard_map/ppermute | solution.py:33
  54.3 4.3 %collective-permute-start.14 = (f32[96,256]{1,0:T(8,128)S(1)}, f32[96,256]{1,0:T(8,128)S(1)}, u32[]{:S(2)}, u32[]{:S(2)}) collective-permute-start(f32[96,256]{1,0:T(8,128)S(1)} %get-tuple-element.45), channel_id=1, source_target_pairs={{0,4},{1,5},{2,6},{3,7},{4,0},{5,1},{6,2},{7,3},{8,12},{9,13},{10,... | collective-permute-start | bytes 294920 | tf_op jit(solution)/shard_map/ppermute | solution.py:33
  58.6 6.5 %collective-permute-done.10.refs_9_ = bf16[2048,128]{1,0:T(8,128)(2,1)S(1)} collective-permute-done((bf16[2048,128]{1,0:T(8,128)(2,1)S(1)}, bf16[2048,128]{1,0:T(8,128)(2,1)S(1)}, u32[]{:S(2)}, u32[]{:S(2)}) %collective-permute-start.10) | collective-permute-done | bytes 524320 | tf_op jit(solution)/shard_map/ppermute | solution.py:33
  66.5 3.8 %shard_map.93 = (f32[64,256]{1,0:T(8,128)S(1)}, f32[64,256]{1,0:T(8,128)S(1)}, bf16[16384,128]{1,0:T(8,128)(2,1)S(1)}) custom-call(bf16[16384,128]{1,0:T(8,128)(2,1)S(1)} %get-tuple-element.37.table, bf16[2048,1664]{1,0:T(8,128)(2,1)S(1)} %get-tuple-element.38.matrix, f32[2048,128]{1,0:T(8,128)S(1)} %get-tuple-element.39.start, ...), custom_call_target="tpu_custom_call", output_to_operand_aliasing={{2}: (0, {})} | custom-call | flops 1073741824 | bytes 17973248 | tf_op jit(solution)/shard_map/pallas_call | solution.py:65
  70.3 2.8 %collective-permute-start.12 = (f32[64,256]{1,0:T(8,128)S(1)}, f32[64,256]{1,0:T(8,128)S(1)}, u32[]{:S(2)}, u32[]{:S(2)}) collective-permute-start(f32[64,256]{1,0:T(8,128)S(1)} %get-tuple-element.42), channel_id=1, source_target_pairs={{0,2},{1,3},{2,0},{3,1},{4,6},{5,7},{6,4},{7,5},{8,10},{9,11},{10,... | collective-permute-start | bytes 196616 | tf_op jit(solution)/shard_map/ppermute | solution.py:33
  73.2 3.3 %collective-permute-done.12.came = f32[64,256]{1,0:T(8,128)S(1)} collective-permute-done((f32[64,256]{1,0:T(8,128)S(1)}, f32[64,256]{1,0:T(8,128)S(1)}, u32[]{:S(2)}, u32[]{:S(2)}) %collective-permute-start.12) | collective-permute-done | bytes 65568 | tf_op jit(solution)/shard_map/ppermute | solution.py:33
  76.5 5.8 %collective-permute-start.16 = (f32[80,256]{1,0:T(8,128)S(1)}, f32[80,256]{1,0:T(8,128)S(1)}, u32[]{:S(2)}, u32[]{:S(2)}) collective-permute-start(f32[80,256]{1,0:T(8,128)S(1)} %get-tuple-element.49), channel_id=1, source_target_pairs={{0,8},{1,9},{2,10},{3,11},{4,12},{5,13},{6,14},{7,15},{8,0},{9,1},... | collective-permute-start | bytes 245768 | tf_op jit(solution)/shard_map/ppermute | solution.py:33
  84.9 5.5 %collective-permute-done.15.one = f32[64,256]{1,0:T(8,128)S(1)} collective-permute-done((f32[64,256]{1,0:T(8,128)S(1)}, f32[64,256]{1,0:T(8,128)S(1)}, u32[]{:S(2)}, u32[]{:S(2)}) %collective-permute-start.15) | collective-permute-done | bytes 65568 | tf_op jit(solution)/shard_map/ppermute | solution.py:33
  90.4 1.4 %collective-permute-done.17.three = f32[64,256]{1,0:T(8,128)S(1)} collective-permute-done((f32[64,256]{1,0:T(8,128)S(1)}, f32[64,256]{1,0:T(8,128)S(1)}, u32[]{:S(2)}, u32[]{:S(2)}) %collective-permute-start.17) | collective-permute-done | bytes 65568 | tf_op jit(solution)/shard_map/ppermute | solution.py:33
  (33 shorter events, 10.5 us)
Async XLA Ops:
  0.6 5.7 %collective-permute-start = (bf16[1024,256]{1,0:T(8,128)(2,1)}, bf16[1024,256]{1,0:T(8,128)(2,1)S(1)}, u32[]{:S(2)}, u32[]{:S(2)}) collective-permute-start(bf16[1024,256]{1,0:T(8,128)(2,1)} %bitcast.10), channel_id=1, source_target_pairs={{0,1},{1,0},{2,3},{3,2},{4,5},{5,4},{6,7},{7,6},{8,9},{9,8},{10,11... | collective-permute-start | bytes 1572872 | tf_op jit(solution)/shard_map/ppermute | solution.py:33
  2.6 20.5 %collective-permute-start.1 = (bf16[1024,1664]{1,0:T(8,128)(2,1)}, bf16[1024,1664]{1,0:T(8,128)(2,1)S(1)}, u32[]{:S(2)}, u32[]{:S(2)}) collective-permute-start(bf16[1024,1664]{1,0:T(8,128)(2,1)} %bitcast.9), channel_id=1, source_target_pairs={{0,1},{1,0},{2,3},{3,2},{4,5},{5,4},{6,7},{7,6},{8,9},{9,8},{10,11... | collective-permute-start | bytes 10223624 | tf_op jit(solution)/shard_map/ppermute | solution.py:33
  5.0 1.0 %copy-start.3 = (bf16[1,1024,256]{2,1,0:T(8,128)(2,1)S(1)}, bf16[1,1024,256]{2,1,0:T(8,128)(2,1)}, u32[]{:S(2)}) copy-start(bf16[1,1024,256]{2,1,0:T(8,128)(2,1)} %param.7) | copy-start | bytes 1572868
  6.7 12.5 %collective-permute-start.3 = (bf16[2048,128]{1,0:T(8,128)(2,1)S(1)}, bf16[2048,128]{1,0:T(8,128)(2,1)S(1)}, u32[]{:S(2)}, u32[]{:S(2)}) collective-permute-start(bf16[2048,128]{1,0:T(8,128)(2,1)S(1)} %get-tuple-element.32.refs_3_), channel_id=1, source_target_pairs={{0,2},{1,15},{2,4},{3,1},{4,6},{5,3},{6,8},{7,5},{8,10},{9,7},{10,... | collective-permute-start | bytes 1572872 | tf_op jit(solution)/shard_map/ppermute | solution.py:33
  10.2 27.3 %collective-permute-start.8 = (bf16[2048,256]{1,0:T(8,128)(2,1)S(1)}, bf16[2048,256]{1,0:T(8,128)(2,1)S(1)}, u32[]{:S(2)}, u32[]{:S(2)}) collective-permute-start(bf16[2048,256]{1,0:T(8,128)(2,1)S(1)} %get-tuple-element.29.both), channel_id=1, source_target_pairs={{0,16},{1,33},{2,18},{3,35},{4,20},{5,37},{6,22},{7,39},{8,24},{9,... | collective-permute-start | bytes 3145736 | tf_op jit(solution)/shard_map/ppermute | solution.py:33
  14.5 13.5 %collective-permute-start.4 = (bf16[2048,128]{1,0:T(8,128)(2,1)S(1)}, bf16[2048,128]{1,0:T(8,128)(2,1)S(1)}, u32[]{:S(2)}, u32[]{:S(2)}) collective-permute-start(bf16[2048,128]{1,0:T(8,128)(2,1)S(1)} %get-tuple-element.32.refs_3_), channel_id=1, source_target_pairs={{0,14},{1,3},{2,0},{3,5},{4,2},{5,7},{6,4},{7,9},{8,6},{9,11},{10,... | collective-permute-start | bytes 1572872 | tf_op jit(solution)/shard_map/ppermute | solution.py:33
  19.2 15.3 %collective-permute-start.5 = (bf16[2048,128]{1,0:T(8,128)(2,1)S(1)}, bf16[2048,128]{1,0:T(8,128)(2,1)S(1)}, u32[]{:S(2)}, u32[]{:S(2)}) collective-permute-start(bf16[2048,128]{1,0:T(8,128)(2,1)S(1)} %collective-permute-done.3.refs_4_), channel_id=1, source_target_pairs={{0,2},{1,15},{2,4},{3,1},{4,6},{5,3},{6,8},{7,5},{8,10},{9,7},{10,... | collective-permute-start | bytes 1572872 | tf_op jit(solution)/shard_map/ppermute | solution.py:33
  23.1 14.3 %collective-permute-start.2 = (f32[1072,128]{1,0:T(8,128)}, f32[1072,128]{1,0:T(8,128)S(1)}, u32[]{:S(2)}, u32[]{:S(2)}) collective-permute-start(f32[1072,128]{1,0:T(8,128)} %shard_map.88.aux), channel_id=1, source_target_pairs={{0,1},{1,0},{2,3},{3,2},{4,5},{5,4},{6,7},{7,6},{8,9},{9,8},{10,11... | collective-permute-start | bytes 1646600 | tf_op jit(solution)/shard_map/ppermute | solution.py:33
  27.9 19.6 %collective-permute-start.6 = (bf16[2048,128]{1,0:T(8,128)(2,1)S(1)}, bf16[2048,128]{1,0:T(8,128)(2,1)S(1)}, u32[]{:S(2)}, u32[]{:S(2)}) collective-permute-start(bf16[2048,128]{1,0:T(8,128)(2,1)S(1)} %collective-permute-done.4.refs_5_), channel_id=1, source_target_pairs={{0,14},{1,3},{2,0},{3,5},{4,2},{5,7},{6,4},{7,9},{8,6},{9,11},{10,... | collective-permute-start | bytes 1572872 | tf_op jit(solution)/shard_map/ppermute | solution.py:33
  34.5 17.8 %collective-permute-start.7 = (bf16[2048,128]{1,0:T(8,128)(2,1)S(1)}, bf16[2048,128]{1,0:T(8,128)(2,1)S(1)}, u32[]{:S(2)}, u32[]{:S(2)}) collective-permute-start(bf16[2048,128]{1,0:T(8,128)(2,1)S(1)} %collective-permute-done.5.refs_6_), channel_id=1, source_target_pairs={{0,2},{1,15},{2,4},{3,1},{4,6},{5,3},{6,8},{7,5},{8,10},{9,7},{10,... | collective-permute-start | bytes 1572872 | tf_op jit(solution)/shard_map/ppermute | solution.py:33
  37.4 1.1 %copy-start = (f32[1072,128]{1,0:T(8,128)S(1)}, f32[1072,128]{1,0:T(8,128)}, u32[]{:S(2)}) copy-start(f32[1072,128]{1,0:T(8,128)} %shard_map.88.aux) | copy-start | bytes 1646596
  40.3 4.8 %collective-permute-start.9 = (f32[128,256]{1,0:T(8,128)S(1)}, f32[128,256]{1,0:T(8,128)S(1)}, u32[]{:S(2)}, u32[]{:S(2)}) collective-permute-start(f32[128,256]{1,0:T(8,128)S(1)} %get-tuple-element.34), channel_id=1, source_target_pairs={{0,1},{1,0},{2,3},{3,2},{4,5},{5,4},{6,7},{7,6},{8,9},{9,8},{10,11... | collective-permute-start | bytes 393224 | tf_op jit(solution)/shard_map/ppermute | solution.py:33
  45.2 9.0 %collective-permute-start.13 = (f32[192,256]{1,0:T(8,128)S(1)}, f32[192,256]{1,0:T(8,128)S(1)}, u32[]{:S(2)}, u32[]{:S(2)}) collective-permute-start(f32[192,256]{1,0:T(8,128)S(1)} %get-tuple-element.35), channel_id=1, source_target_pairs={{0,2},{1,3},{2,0},{3,1},{4,6},{5,7},{6,4},{7,5},{8,10},{9,11},{10,... | collective-permute-start | bytes 589832 | tf_op jit(solution)/shard_map/ppermute | solution.py:33
  47.6 17.5 %collective-permute-start.10 = (bf16[2048,128]{1,0:T(8,128)(2,1)S(1)}, bf16[2048,128]{1,0:T(8,128)(2,1)S(1)}, u32[]{:S(2)}, u32[]{:S(2)}) collective-permute-start(bf16[2048,128]{1,0:T(8,128)(2,1)S(1)} %collective-permute-done.6.refs_7_), channel_id=1, source_target_pairs={{0,14},{1,3},{2,0},{3,5},{4,2},{5,7},{6,4},{7,9},{8,6},{9,11},{10,... | collective-permute-start | bytes 1572872 | tf_op jit(solution)/shard_map/ppermute | solution.py:33
  52.3 14.2 %collective-permute-start.11 = (bf16[2048,128]{1,0:T(8,128)(2,1)S(1)}, bf16[2048,128]{1,0:T(8,128)(2,1)S(1)}, u32[]{:S(2)}, u32[]{:S(2)}) collective-permute-start(bf16[2048,128]{1,0:T(8,128)(2,1)S(1)} %collective-permute-done.7.refs_8_), channel_id=1, source_target_pairs={{0,2},{1,15},{2,4},{3,1},{4,6},{5,3},{6,8},{7,5},{8,10},{9,7},{10,... | collective-permute-start | bytes 1572872 | tf_op jit(solution)/shard_map/ppermute | solution.py:33
  54.2 10.8 %copy-start.1 = (f32[1072,128]{1,0:T(8,128)S(1)}, f32[1072,128]{1,0:T(8,128)}, u32[]{:S(2)}) copy-start(f32[1072,128]{1,0:T(8,128)} %shard_map.88.aux) | copy-start | bytes 1646596
  54.2 10.8 %copy-start.2 = (bf16[1,1024,1664]{2,1,0:T(8,128)(2,1)S(1)}, bf16[1,1024,1664]{2,1,0:T(8,128)(2,1)}, u32[]{:S(2)}) copy-start(bf16[1,1024,1664]{2,1,0:T(8,128)(2,1)} %refs_1_.1) | copy-start | bytes 10223620
  54.3 10.8 %copy-start.4 = (s32[1,16,26]{2,1,0:T(8,128)S(1)}, s32[1,16,26]{2,1,0:T(8,128)}, u32[]{:S(2)}) copy-start(s32[1,16,26]{2,1,0:T(8,128)} %refs_0_.1) | copy-start | bytes 4996
  54.3 18.8 %collective-permute-start.14 = (f32[96,256]{1,0:T(8,128)S(1)}, f32[96,256]{1,0:T(8,128)S(1)}, u32[]{:S(2)}, u32[]{:S(2)}) collective-permute-start(f32[96,256]{1,0:T(8,128)S(1)} %get-tuple-element.45), channel_id=1, source_target_pairs={{0,4},{1,5},{2,6},{3,7},{4,0},{5,1},{6,2},{7,3},{8,12},{9,13},{10,... | collective-permute-start | bytes 294920 | tf_op jit(solution)/shard_map/ppermute | solution.py:33
  70.3 6.2 %collective-permute-start.12 = (f32[64,256]{1,0:T(8,128)S(1)}, f32[64,256]{1,0:T(8,128)S(1)}, u32[]{:S(2)}, u32[]{:S(2)}) collective-permute-start(f32[64,256]{1,0:T(8,128)S(1)} %get-tuple-element.42), channel_id=1, source_target_pairs={{0,2},{1,3},{2,0},{3,1},{4,6},{5,7},{6,4},{7,5},{8,10},{9,11},{10,... | collective-permute-start | bytes 196616 | tf_op jit(solution)/shard_map/ppermute | solution.py:33
  76.5 15.4 %collective-permute-start.16 = (f32[80,256]{1,0:T(8,128)S(1)}, f32[80,256]{1,0:T(8,128)S(1)}, u32[]{:S(2)}, u32[]{:S(2)}) collective-permute-start(f32[80,256]{1,0:T(8,128)S(1)} %get-tuple-element.49), channel_id=1, source_target_pairs={{0,8},{1,9},{2,10},{3,11},{4,12},{5,13},{6,14},{7,15},{8,0},{9,1},... | collective-permute-start | bytes 245768 | tf_op jit(solution)/shard_map/ppermute | solution.py:33
  82.3 8.1 %collective-permute-start.15 = (f32[64,256]{1,0:T(8,128)S(1)}, f32[64,256]{1,0:T(8,128)S(1)}, u32[]{:S(2)}, u32[]{:S(2)}) collective-permute-start(f32[64,256]{1,0:T(8,128)S(1)} %get-tuple-element.48), channel_id=1, source_target_pairs={{4,0},{5,1},{6,2},{7,3},{16,20},{17,21},{18,22},{19,23},{44,40},{4... | collective-permute-start | bytes 196616 | tf_op jit(solution)/shard_map/ppermute | solution.py:33
  83.6 8.3 %collective-permute-start.17 = (f32[64,256]{1,0:T(8,128)S(1)}, f32[64,256]{1,0:T(8,128)S(1)}, u32[]{:S(2)}, u32[]{:S(2)}) collective-permute-start(f32[64,256]{1,0:T(8,128)S(1)} %get-tuple-element.48), channel_id=1, source_target_pairs={{12,0},{13,1},{14,2},{15,3},{24,20},{25,21},{26,22},{27,23},{36,40... | collective-permute-start | bytes 196616 | tf_op jit(solution)/shard_map/ppermute | solution.py:33

commit v4 on v3

--- a/solution.py
+++ b/solution.py
@@ -143,26 +143,25 @@
             )
 
 
-def mass_kernel(both, aux, aux_other, mred, weights):
+def mass_kernel(both, aux, aux_other, mred, masked, spots, weights):
     _, _, core = place()
     spread(weights, aux[MASS : MASS + 8, :], aux_other[MASS : MASS + 8, :])
     pick = mine_of(256, lambda n: 64 * ((n % 64) // 16) + 32 * (n // 64) + 16 * core + n % 16)
     weighted = (weights[...] * dot(both[...], pick)).astype(BF16)
     mred[...] = dot_t(weighted, both[...])
-
-
-def early_kernel(both, aux, aux_other, partner, to_send, to_keep, coupled, masked, spots, at, sem):
-    _, _, core = place()
     spots[...] = jnp.zeros((8, 128), jnp.int32)
+    here = lax.broadcasted_iota(jnp.int32, (1024, 128), 1) // BLK == core
     for part, rows in enumerate((aux, aux_other)):
         links = rows[LINKS : LINKS + 2, 0:16].astype(jnp.int32)
         spots[part : part + 1, 0:16] = part * 1024 + jnp.where(core == 0, links[0:1, :], links[1:2, :]) * BLK
+        couple = rows[COUPLE : COUPLE + 1024, :]
+        masked[part * 1024 : (part + 1) * 1024, :] = jnp.where(here, couple, 0.0).astype(BF16)
+
+
+def early_kernel(both, partner, mred, masked, spots, to_send, to_keep, coupled, at, sem):
+    _, side, _ = place()
     copy = pltpu.make_async_copy(spots, at, sem)
     copy.start()
-    mine = lax.broadcasted_iota(jnp.int32, (1024, 128), 1) // BLK == core
-    for part, rows in enumerate((aux, aux_other)):
-        couple = rows[COUPLE : COUPLE + 1024, :]
-        masked[part * 1024 : (part + 1) * 1024, :] = jnp.where(mine, couple, 0.0).astype(BF16)
     copy.wait()
 
     def one(b, carry):
@@ -173,28 +172,28 @@
 
     lax.fori_loop(0, 32, one, 0, unroll=16)
     term = dot_t(coupled[...], both[...])
-    for k in range(2):
-        low, high = term[k * 128 : k * 128 + 64, :], term[k * 128 + 64 : k * 128 + 128, :]
-        to_keep[k * 64 : (k + 1) * 64, :] = jnp.where(core == 0, low, high)
-        to_send[k * 64 : (k + 1) * 64, :] = jnp.where(core == 0, high, low)
-
-
-def turn_kernel(kept, came, mred, to_send, to_keep):
-    _, side, core = place()
-    sib = jnp.where(core == 0, kept[...], came[...])
-    cous = jnp.where(core == 0, came[...], kept[...])
-    for t, term in enumerate((sib, cous, mred[...])):
-        low, high = term[0:64, :], term[64:128, :]
-        to_send[t * 64 : (t + 1) * 64, :] = jnp.where(side == 0, high, low)
-        to_keep[t * 64 : (t + 1) * 64, :] = jnp.where(side == 0, low, high)
+    for low, high, rows in (
+        (term[0:128, :], term[128:256, :], slice(0, 128)),
+        (mred[0:64, :], mred[64:128, :], slice(128, 192)),
+    ):
+        to_send[rows, :] = jnp.where(side == 0, high, low)
+        to_keep[rows, :] = jnp.where(side == 0, low, high)
+
+
+def turn_kernel(kept, came, to_send, to_keep):
+    _, _, core = place()
+    total = kept[...] + came[...]
+    to_send[...] = jnp.where(core == 0, total[64:128, :], total[0:64, :])
+    to_keep[0:64, :] = jnp.where(core == 0, total[0:64, :], total[64:128, :])
+    to_keep[64:128, :] = total[128:192, :]
 
 
 def split_kernel(kept, came, to_send, to_keep):
-    group, _, _ = place()
+    group, _, core = place()
     odd = (group ^ (lax.axis_index("leaf") % 4)) % 2 == 1
-    sib = kept[0:64, :] + came[0:64, :]
-    cous = kept[64:128, :] + came[64:128, :]
-    mass = kept[128:192, :] + came[128:192, :]
+    sib = jnp.where(core == 0, kept[0:64, :], came[...])
+    cous = jnp.where(core == 0, came[...], kept[0:64, :])
+    mass = kept[64:128, :]
     to_keep[0:64, :] = jnp.where(odd, sib, cous)
     to_send[0:64, :] = jnp.where(odd, cous, sib)
     low = group % 2 == 0
@@ -308,31 +307,29 @@
     partner = send(both, lambda leaf, row: (leaf ^ (1 + row % 2), row))
     stiff_other = send(stiff[0], to_core)
     aux_other = send(after(aux, stiff_other), to_core)
-    (mass_part,) = call(
-        mass_kernel, [shape(128, 256)], [both, aux, aux_other], [], [pltpu.VMEM((2048, 128), F32)], 0
+    mass_part, masked, spots = call(
+        mass_kernel,
+        [shape(128, 256), shape(2048, 128, dtype=BF16), shape(8, 128, dtype=jnp.int32)],
+        [both, aux, aux_other],
+        [],
+        [pltpu.VMEM((2048, 128), F32)],
     )
     left2, right2 = send(left1, ring(True)), send(right1, ring(False))
     go, keep = call(
         early_kernel,
-        [shape(128, 256)] * 2,
-        [both, aux, aux_other, partner],
+        [shape(192, 256)] * 2,
+        [both, partner, mass_part, masked, spots],
         [],
-        [
-            pltpu.VMEM((2048, 256), BF16),
-            pltpu.VMEM((2048, 128), BF16),
-            pltpu.VMEM((8, 128), jnp.int32),
-            pltpu.SMEM((8, 128), jnp.int32),
-            pltpu.SemaphoreType.DMA,
-        ],
+        [pltpu.VMEM((2048, 256), BF16), pltpu.SMEM((8, 128), jnp.int32), pltpu.SemaphoreType.DMA],
         flops=2**30,
         vmem=16,
     )
-    came = send(go, to_core)
-    go, keep = call(turn_kernel, [shape(192, 256)] * 2, [keep, came, mass_part])
     left3, right3 = send(left2, ring(True)), send(after(right2, go), ring(False))
     left4 = send(left3, ring(True))
     came = send(go, to_side)
-    go, early_keep = call(split_kernel, [shape(96, 256)] * 2, [keep, came], flops=5 * 10**9)
+    go, keep = call(turn_kernel, [shape(64, 256), shape(128, 256)], [keep, came], flops=0 * 10**9)
+    came = send(go, to_core)
+    go, early_keep = call(split_kernel, [shape(96, 256)] * 2, [keep, came], flops=4 * 10**9)
     early_came = send(go, to_group(1))
 
     table, matrix, start, spots = call(

time: 94.2 us -> 92.2 us (0.979); the launches traced: 92.5 us -> 91.5 us
  waiting for transfers between devices: 22.3 us -> 15.6 us
  starting transfers between devices: 55.9 us -> 61.6 us
    ppermute x18, waiting for transfers between devices: 22.3 us -> 15.6 us  [send(): return lax.ppermute(value, ('leaf', 'rows'), pairs)]
    ppermute x18, starting transfers between devices: 55.9 us -> 61.6 us  [send(): return lax.ppermute(value, ('leaf', 'rows'), pairs)]
  transfers between devices with their start and end apart: 18 -> 18, of which waited for: 7 -> 7; matrix products, arithmetic and copies ran while one was open for 0% -> 0% of each run, Pallas kernels for 11% -> 12%
where the time goes in v4:
time: 92.2 us; the launch traced here: 91.5 us
  starting transfers between devices  61.6 us (67%)
  waiting for transfers between devices  15.6 us (17%)
  Pallas kernels  11.3 us (12%)
  local copies, waits for them, and re-layouts  2.09 us (2%)
  between operations  0.96 us (1%)
    ppermute x18, starting transfers between devices, send(): return lax.ppermute(value, ('leaf', 'rows'), pairs)  61.6 us
    ppermute x18, waiting for transfers between devices, send(): return lax.ppermute(value, ('leaf', 'rows'), pairs)  15.6 us
    pallas_call x11, Pallas kernels, call(): pl.pallas_call(body, out_shape=outs, in_specs=[VMEM] * len(arrays) + [HBM...  11.3 us
    unnamed x10, local copies, waits for them, and re-layouts  2.09 us
  transfers between devices with their start and end apart: 18, of which 7 were waited for; matrix products, arithmetic and copies ran while one was open for 0% of the time, Pallas kernels for 12%

profile of v4, /device:TPU:6, one launch (start us, length us, event | category | flops | bytes accessed | tf_op | source)
XLA Modules:
  0.0 91.5 jit_solution(10163914724281873839)
XLA Ops:
  0.6 1.9 %collective-permute-start = (bf16[1024,256]{1,0:T(8,128)(2,1)}, bf16[1024,256]{1,0:T(8,128)(2,1)S(1)}, u32[]{:S(2)}, u32[]{:S(2)}) collective-permute-start(bf16[1024,256]{1,0:T(8,128)(2,1)} %bitcast.10), channel_id=1, source_target_pairs={{0,1},{1,0},{2,3},{3,2},{4,5},{5,4},{6,7},{7,6},{8,9},{9,8},{10,11... | collective-permute-start | bytes 1572872 | tf_op jit(solution)/shard_map/ppermute | solution.py:33
  2.6 2.4 %collective-permute-start.1 = (bf16[1024,1664]{1,0:T(8,128)(2,1)}, bf16[1024,1664]{1,0:T(8,128)(2,1)S(1)}, u32[]{:S(2)}, u32[]{:S(2)}) collective-permute-start(bf16[1024,1664]{1,0:T(8,128)(2,1)} %bitcast.9), channel_id=1, source_target_pairs={{0,1},{1,0},{2,3},{3,2},{4,5},{5,4},{6,7},{7,6},{8,9},{9,8},{10,11... | collective-permute-start | bytes 10223624 | tf_op jit(solution)/shard_map/ppermute | solution.py:33
  6.7 3.5 %collective-permute-start.3 = (bf16[2048,128]{1,0:T(8,128)(2,1)S(1)}, bf16[2048,128]{1,0:T(8,128)(2,1)S(1)}, u32[]{:S(2)}, u32[]{:S(2)}) collective-permute-start(bf16[2048,128]{1,0:T(8,128)(2,1)S(1)} %get-tuple-element.35.refs_3_), channel_id=1, source_target_pairs={{0,2},{1,15},{2,4},{3,1},{4,6},{5,3},{6,8},{7,5},{8,10},{9,7},{10,... | collective-permute-start | bytes 1572872 | tf_op jit(solution)/shard_map/ppermute | solution.py:33
  10.2 4.3 %collective-permute-start.8 = (bf16[2048,256]{1,0:T(8,128)(2,1)S(1)}, bf16[2048,256]{1,0:T(8,128)(2,1)S(1)}, u32[]{:S(2)}, u32[]{:S(2)}) collective-permute-start(bf16[2048,256]{1,0:T(8,128)(2,1)S(1)} %get-tuple-element.32.both), channel_id=1, source_target_pairs={{0,16},{1,33},{2,18},{3,35},{4,20},{5,37},{6,22},{7,39},{8,24},{9,... | collective-permute-start | bytes 3145736 | tf_op jit(solution)/shard_map/ppermute | solution.py:33
  14.5 3.8 %collective-permute-start.4 = (bf16[2048,128]{1,0:T(8,128)(2,1)S(1)}, bf16[2048,128]{1,0:T(8,128)(2,1)S(1)}, u32[]{:S(2)}, u32[]{:S(2)}) collective-permute-start(bf16[2048,128]{1,0:T(8,128)(2,1)S(1)} %get-tuple-element.35.refs_3_), channel_id=1, source_target_pairs={{0,14},{1,3},{2,0},{3,5},{4,2},{5,7},{6,4},{7,9},{8,6},{9,11},{10,... | collective-permute-start | bytes 1572872 | tf_op jit(solution)/shard_map/ppermute | solution.py:33
  19.2 2.0 %collective-permute-start.5 = (bf16[2048,128]{1,0:T(8,128)(2,1)S(1)}, bf16[2048,128]{1,0:T(8,128)(2,1)S(1)}, u32[]{:S(2)}, u32[]{:S(2)}) collective-permute-start(bf16[2048,128]{1,0:T(8,128)(2,1)S(1)} %collective-permute-done.3.refs_4_), channel_id=1, source_target_pairs={{0,2},{1,15},{2,4},{3,1},{4,6},{5,3},{6,8},{7,5},{8,10},{9,7},{10,... | collective-permute-start | bytes 1572872 | tf_op jit(solution)/shard_map/ppermute | solution.py:33
  21.2 1.8 %shard_map.88.aux = f32[1072,128]{1,0:T(8,128)} custom-call(bf16[1,1024,128]{2,1,0:T(8,128)(2,1)} %couple_at.1, s32[1,16,26]{2,1,0:T(8,128)} %refs_0_.1, s32[1,2,16]{2,1,0:T(2,128)} %bitcast.12, f32[1,1024]{1,0:T(1,128)} %shift_at.1, f32[1,1024]{1,0:T(1,128)} %mass_at.1), custom_call_target="tpu_custom_call" | custom-call | bytes 820992 | tf_op jit(solution)/shard_map/pallas_call | solution.py:65
  23.1 4.8 %collective-permute-start.2 = (f32[1072,128]{1,0:T(8,128)}, f32[1072,128]{1,0:T(8,128)S(1)}, u32[]{:S(2)}, u32[]{:S(2)}) collective-permute-start(f32[1072,128]{1,0:T(8,128)} %shard_map.88.aux), channel_id=1, source_target_pairs={{0,1},{1,0},{2,3},{3,2},{4,5},{5,4},{6,7},{7,6},{8,9},{9,8},{10,11... | collective-permute-start | bytes 1646600 | tf_op jit(solution)/shard_map/ppermute | solution.py:33
  27.9 3.1 %collective-permute-start.6 = (bf16[2048,128]{1,0:T(8,128)(2,1)S(1)}, bf16[2048,128]{1,0:T(8,128)(2,1)S(1)}, u32[]{:S(2)}, u32[]{:S(2)}) collective-permute-start(bf16[2048,128]{1,0:T(8,128)(2,1)S(1)} %collective-permute-done.4.refs_5_), channel_id=1, source_target_pairs={{0,14},{1,3},{2,0},{3,5},{4,2},{5,7},{6,4},{7,9},{8,6},{9,11},{10,... | collective-permute-start | bytes 1572872 | tf_op jit(solution)/shard_map/ppermute | solution.py:33
  31.0 3.5 %collective-permute-done.5.refs_6_ = bf16[2048,128]{1,0:T(8,128)(2,1)S(1)} collective-permute-done((bf16[2048,128]{1,0:T(8,128)(2,1)S(1)}, bf16[2048,128]{1,0:T(8,128)(2,1)S(1)}, u32[]{:S(2)}, u32[]{:S(2)}) %collective-permute-start.5) | collective-permute-done | bytes 524320 | tf_op jit(solution)/shard_map/ppermute | solution.py:33
  34.5 1.9 %collective-permute-start.7 = (bf16[2048,128]{1,0:T(8,128)(2,1)S(1)}, bf16[2048,128]{1,0:T(8,128)(2,1)S(1)}, u32[]{:S(2)}, u32[]{:S(2)}) collective-permute-start(bf16[2048,128]{1,0:T(8,128)(2,1)S(1)} %collective-permute-done.5.refs_6_), channel_id=1, source_target_pairs={{0,2},{1,15},{2,4},{3,1},{4,6},{5,3},{6,8},{7,5},{8,10},{9,7},{10,... | collective-permute-start | bytes 1572872 | tf_op jit(solution)/shard_map/ppermute | solution.py:33
  38.6 1.8 %shard_map.90 = (f32[192,256]{1,0:T(8,128)S(1)}, f32[192,256]{1,0:T(8,128)S(1)}) custom-call(bf16[2048,256]{1,0:T(8,128)(2,1)S(1)} %get-tuple-element.32.both, bf16[2048,256]{1,0:T(8,128)(2,1)S(1)} %collective-permute-done.8.partner, f32[128,256]{1,0:T(8,128)S(1)} %get-tuple-element.36.mred, bf16[2048,128]{1,0:T(8,128)(2,1)S(1)} %get-tuple-element.37.masked, ...), custom_call_target="tpu_custom_call" | custom-call | flops 1073741824 | bytes 3149824 | tf_op jit(solution)/shard_map/pallas_call | solution.py:65
  40.4 2.8 %collective-permute-start.12 = (f32[192,256]{1,0:T(8,128)S(1)}, f32[192,256]{1,0:T(8,128)S(1)}, u32[]{:S(2)}, u32[]{:S(2)}) collective-permute-start(f32[192,256]{1,0:T(8,128)S(1)} %get-tuple-element.39), channel_id=1, source_target_pairs={{0,2},{1,3},{2,0},{3,1},{4,6},{5,7},{6,4},{7,5},{8,10},{9,11},{10,... | collective-permute-start | bytes 589832 | tf_op jit(solution)/shard_map/ppermute | solution.py:33
  43.2 4.7 %collective-permute-start.9 = (bf16[2048,128]{1,0:T(8,128)(2,1)S(1)}, bf16[2048,128]{1,0:T(8,128)(2,1)S(1)}, u32[]{:S(2)}, u32[]{:S(2)}) collective-permute-start(bf16[2048,128]{1,0:T(8,128)(2,1)S(1)} %collective-permute-done.6.refs_7_), channel_id=1, source_target_pairs={{0,14},{1,3},{2,0},{3,5},{4,2},{5,7},{6,4},{7,9},{8,6},{9,11},{10,... | collective-permute-start | bytes 1572872 | tf_op jit(solution)/shard_map/ppermute | solution.py:33
  48.9 1.9 %collective-permute-start.10 = (bf16[2048,128]{1,0:T(8,128)(2,1)S(1)}, bf16[2048,128]{1,0:T(8,128)(2,1)S(1)}, u32[]{:S(2)}, u32[]{:S(2)}) collective-permute-start(bf16[2048,128]{1,0:T(8,128)(2,1)S(1)} %collective-permute-done.7.refs_8_), channel_id=1, source_target_pairs={{0,2},{1,15},{2,4},{3,1},{4,6},{5,3},{6,8},{7,5},{8,10},{9,7},{10,... | collective-permute-start | bytes 1572872 | tf_op jit(solution)/shard_map/ppermute | solution.py:33
  50.9 3.1 %collective-permute-start.13 = (f32[64,256]{1,0:T(8,128)S(1)}, f32[64,256]{1,0:T(8,128)S(1)}, u32[]{:S(2)}, u32[]{:S(2)}) collective-permute-start(f32[64,256]{1,0:T(8,128)S(1)} %get-tuple-element.49), channel_id=1, source_target_pairs={{0,1},{1,0},{2,3},{3,2},{4,5},{5,4},{6,7},{7,6},{8,9},{9,8},{10,11... | collective-permute-start | bytes 196616 | tf_op jit(solution)/shard_map/ppermute | solution.py:33
  54.9 6.2 %collective-permute-start.14 = (f32[96,256]{1,0:T(8,128)S(1)}, f32[96,256]{1,0:T(8,128)S(1)}, u32[]{:S(2)}, u32[]{:S(2)}) collective-permute-start(f32[96,256]{1,0:T(8,128)S(1)} %get-tuple-element.51), channel_id=1, source_target_pairs={{0,4},{1,5},{2,6},{3,7},{4,0},{5,1},{6,2},{7,3},{8,12},{9,13},{10,... | collective-permute-start | bytes 294920 | tf_op jit(solution)/shard_map/ppermute | solution.py:33
  61.2 1.4 %shard_map.91 = (bf16[16384,128]{1,0:T(8,128)(2,1)S(1)}, bf16[2048,1664]{1,0:T(8,128)(2,1)S(1)}, f32[2048,128]{1,0:T(8,128)S(1)}, s32[32,128]{1,0:T(8,128)S(1)}) custom-call(bf16[2048,256]{1,0:T(8,128)(2,1)S(1)} %get-tuple-element.32.both, f32[1072,128]{1,0:T(8,128)S(1)} %copy-done.1, f32[1072,128]{1,0:T(8,128)S(1)} %collective-permute-done.2.aux_other, ...), custom_call_target="tpu_custom_call" | custom-call | bytes 24708736 | tf_op jit(solution)/shard_map/pallas_call | solution.py:65
  62.6 3.8 %shard_map.92 = (f32[64,256]{1,0:T(8,128)S(1)}, f32[64,256]{1,0:T(8,128)S(1)}, bf16[16384,128]{1,0:T(8,128)(2,1)S(1)}) custom-call(bf16[16384,128]{1,0:T(8,128)(2,1)S(1)} %get-tuple-element.41.table, bf16[2048,1664]{1,0:T(8,128)(2,1)S(1)} %get-tuple-element.42.matrix, f32[2048,128]{1,0:T(8,128)S(1)} %get-tuple-element.43.start, ...), custom_call_target="tpu_custom_call", output_to_operand_aliasing={{2}: (0, {})} | custom-call | flops 1073741824 | bytes 17973248 | tf_op jit(solution)/shard_map/pallas_call | solution.py:65
  66.4 5.1 %collective-permute-start.11 = (f32[64,256]{1,0:T(8,128)S(1)}, f32[64,256]{1,0:T(8,128)S(1)}, u32[]{:S(2)}, u32[]{:S(2)}) collective-permute-start(f32[64,256]{1,0:T(8,128)S(1)} %get-tuple-element.46), channel_id=1, source_target_pairs={{0,2},{1,3},{2,0},{3,1},{4,6},{5,7},{6,4},{7,5},{8,10},{9,11},{10,... | collective-permute-start | bytes 196616 | tf_op jit(solution)/shard_map/ppermute | solution.py:33
  71.5 2.2 %collective-permute-done.11.came = f32[64,256]{1,0:T(8,128)S(1)} collective-permute-done((f32[64,256]{1,0:T(8,128)S(1)}, f32[64,256]{1,0:T(8,128)S(1)}, u32[]{:S(2)}, u32[]{:S(2)}) %collective-permute-start.11) | collective-permute-done | bytes 65568 | tf_op jit(solution)/shard_map/ppermute | solution.py:33
  73.8 7.5 %collective-permute-start.16 = (f32[80,256]{1,0:T(8,128)S(1)}, f32[80,256]{1,0:T(8,128)S(1)}, u32[]{:S(2)}, u32[]{:S(2)}) collective-permute-start(f32[80,256]{1,0:T(8,128)S(1)} %get-tuple-element.55), channel_id=1, source_target_pairs={{0,8},{1,9},{2,10},{3,11},{4,12},{5,13},{6,14},{7,15},{8,0},{9,1},... | collective-permute-start | bytes 245768 | tf_op jit(solution)/shard_map/ppermute | solution.py:33
  83.9 4.6 %collective-permute-done.15.one = f32[64,256]{1,0:T(8,128)S(1)} collective-permute-done((f32[64,256]{1,0:T(8,128)S(1)}, f32[64,256]{1,0:T(8,128)S(1)}, u32[]{:S(2)}, u32[]{:S(2)}) %collective-permute-start.15) | collective-permute-done | bytes 65568 | tf_op jit(solution)/shard_map/ppermute | solution.py:33
  88.5 2.4 %collective-permute-done.17.three = f32[64,256]{1,0:T(8,128)S(1)} collective-permute-done((f32[64,256]{1,0:T(8,128)S(1)}, f32[64,256]{1,0:T(8,128)S(1)}, u32[]{:S(2)}, u32[]{:S(2)}) %collective-permute-start.17) | collective-permute-done | bytes 65568 | tf_op jit(solution)/shard_map/ppermute | solution.py:33
  (33 shorter events, 10.0 us)
Async XLA Ops:
  0.6 5.7 %collective-permute-start = (bf16[1024,256]{1,0:T(8,128)(2,1)}, bf16[1024,256]{1,0:T(8,128)(2,1)S(1)}, u32[]{:S(2)}, u32[]{:S(2)}) collective-permute-start(bf16[1024,256]{1,0:T(8,128)(2,1)} %bitcast.10), channel_id=1, source_target_pairs={{0,1},{1,0},{2,3},{3,2},{4,5},{5,4},{6,7},{7,6},{8,9},{9,8},{10,11... | collective-permute-start | bytes 1572872 | tf_op jit(solution)/shard_map/ppermute | solution.py:33
  2.6 20.5 %collective-permute-start.1 = (bf16[1024,1664]{1,0:T(8,128)(2,1)}, bf16[1024,1664]{1,0:T(8,128)(2,1)S(1)}, u32[]{:S(2)}, u32[]{:S(2)}) collective-permute-start(bf16[1024,1664]{1,0:T(8,128)(2,1)} %bitcast.9), channel_id=1, source_target_pairs={{0,1},{1,0},{2,3},{3,2},{4,5},{5,4},{6,7},{7,6},{8,9},{9,8},{10,11... | collective-permute-start | bytes 10223624 | tf_op jit(solution)/shard_map/ppermute | solution.py:33
  5.0 1.0 %copy-start.3 = (bf16[1,1024,256]{2,1,0:T(8,128)(2,1)S(1)}, bf16[1,1024,256]{2,1,0:T(8,128)(2,1)}, u32[]{:S(2)}) copy-start(bf16[1,1024,256]{2,1,0:T(8,128)(2,1)} %param.7) | copy-start | bytes 1572868
  6.7 12.5 %collective-permute-start.3 = (bf16[2048,128]{1,0:T(8,128)(2,1)S(1)}, bf16[2048,128]{1,0:T(8,128)(2,1)S(1)}, u32[]{:S(2)}, u32[]{:S(2)}) collective-permute-start(bf16[2048,128]{1,0:T(8,128)(2,1)S(1)} %get-tuple-element.35.refs_3_), channel_id=1, source_target_pairs={{0,2},{1,15},{2,4},{3,1},{4,6},{5,3},{6,8},{7,5},{8,10},{9,7},{10,... | collective-permute-start | bytes 1572872 | tf_op jit(solution)/shard_map/ppermute | solution.py:33
  10.2 28.5 %collective-permute-start.8 = (bf16[2048,256]{1,0:T(8,128)(2,1)S(1)}, bf16[2048,256]{1,0:T(8,128)(2,1)S(1)}, u32[]{:S(2)}, u32[]{:S(2)}) collective-permute-start(bf16[2048,256]{1,0:T(8,128)(2,1)S(1)} %get-tuple-element.32.both), channel_id=1, source_target_pairs={{0,16},{1,33},{2,18},{3,35},{4,20},{5,37},{6,22},{7,39},{8,24},{9,... | collective-permute-start | bytes 3145736 | tf_op jit(solution)/shard_map/ppermute | solution.py:33
  14.5 13.5 %collective-permute-start.4 = (bf16[2048,128]{1,0:T(8,128)(2,1)S(1)}, bf16[2048,128]{1,0:T(8,128)(2,1)S(1)}, u32[]{:S(2)}, u32[]{:S(2)}) collective-permute-start(bf16[2048,128]{1,0:T(8,128)(2,1)S(1)} %get-tuple-element.35.refs_3_), channel_id=1, source_target_pairs={{0,14},{1,3},{2,0},{3,5},{4,2},{5,7},{6,4},{7,9},{8,6},{9,11},{10,... | collective-permute-start | bytes 1572872 | tf_op jit(solution)/shard_map/ppermute | solution.py:33
  19.2 15.3 %collective-permute-start.5 = (bf16[2048,128]{1,0:T(8,128)(2,1)S(1)}, bf16[2048,128]{1,0:T(8,128)(2,1)S(1)}, u32[]{:S(2)}, u32[]{:S(2)}) collective-permute-start(bf16[2048,128]{1,0:T(8,128)(2,1)S(1)} %collective-permute-done.3.refs_4_), channel_id=1, source_target_pairs={{0,2},{1,15},{2,4},{3,1},{4,6},{5,3},{6,8},{7,5},{8,10},{9,7},{10,... | collective-permute-start | bytes 1572872 | tf_op jit(solution)/shard_map/ppermute | solution.py:33
  23.1 13.4 %collective-permute-start.2 = (f32[1072,128]{1,0:T(8,128)}, f32[1072,128]{1,0:T(8,128)S(1)}, u32[]{:S(2)}, u32[]{:S(2)}) collective-permute-start(f32[1072,128]{1,0:T(8,128)} %shard_map.88.aux), channel_id=1, source_target_pairs={{0,1},{1,0},{2,3},{3,2},{4,5},{5,4},{6,7},{7,6},{8,9},{9,8},{10,11... | collective-permute-start | bytes 1646600 | tf_op jit(solution)/shard_map/ppermute | solution.py:33
  27.9 15.3 %collective-permute-start.6 = (bf16[2048,128]{1,0:T(8,128)(2,1)S(1)}, bf16[2048,128]{1,0:T(8,128)(2,1)S(1)}, u32[]{:S(2)}, u32[]{:S(2)}) collective-permute-start(bf16[2048,128]{1,0:T(8,128)(2,1)S(1)} %collective-permute-done.4.refs_5_), channel_id=1, source_target_pairs={{0,14},{1,3},{2,0},{3,5},{4,2},{5,7},{6,4},{7,9},{8,6},{9,11},{10,... | collective-permute-start | bytes 1572872 | tf_op jit(solution)/shard_map/ppermute | solution.py:33
  34.5 14.4 %collective-permute-start.7 = (bf16[2048,128]{1,0:T(8,128)(2,1)S(1)}, bf16[2048,128]{1,0:T(8,128)(2,1)S(1)}, u32[]{:S(2)}, u32[]{:S(2)}) collective-permute-start(bf16[2048,128]{1,0:T(8,128)(2,1)S(1)} %collective-permute-done.5.refs_6_), channel_id=1, source_target_pairs={{0,2},{1,15},{2,4},{3,1},{4,6},{5,3},{6,8},{7,5},{8,10},{9,7},{10,... | collective-permute-start | bytes 1572872 | tf_op jit(solution)/shard_map/ppermute | solution.py:33
  36.5 1.1 %copy-start = (f32[1072,128]{1,0:T(8,128)S(1)}, f32[1072,128]{1,0:T(8,128)}, u32[]{:S(2)}) copy-start(f32[1072,128]{1,0:T(8,128)} %shard_map.88.aux) | copy-start | bytes 1646596
  40.4 10.5 %collective-permute-start.12 = (f32[192,256]{1,0:T(8,128)S(1)}, f32[192,256]{1,0:T(8,128)S(1)}, u32[]{:S(2)}, u32[]{:S(2)}) collective-permute-start(f32[192,256]{1,0:T(8,128)S(1)} %get-tuple-element.39), channel_id=1, source_target_pairs={{0,2},{1,3},{2,0},{3,1},{4,6},{5,7},{6,4},{7,5},{8,10},{9,11},{10,... | collective-permute-start | bytes 589832 | tf_op jit(solution)/shard_map/ppermute | solution.py:33
  43.2 17.9 %collective-permute-start.9 = (bf16[2048,128]{1,0:T(8,128)(2,1)S(1)}, bf16[2048,128]{1,0:T(8,128)(2,1)S(1)}, u32[]{:S(2)}, u32[]{:S(2)}) collective-permute-start(bf16[2048,128]{1,0:T(8,128)(2,1)S(1)} %collective-permute-done.6.refs_7_), channel_id=1, source_target_pairs={{0,14},{1,3},{2,0},{3,5},{4,2},{5,7},{6,4},{7,9},{8,6},{9,11},{10,... | collective-permute-start | bytes 1572872 | tf_op jit(solution)/shard_map/ppermute | solution.py:33
  48.9 13.6 %collective-permute-start.10 = (bf16[2048,128]{1,0:T(8,128)(2,1)S(1)}, bf16[2048,128]{1,0:T(8,128)(2,1)S(1)}, u32[]{:S(2)}, u32[]{:S(2)}) collective-permute-start(bf16[2048,128]{1,0:T(8,128)(2,1)S(1)} %collective-permute-done.7.refs_8_), channel_id=1, source_target_pairs={{0,2},{1,15},{2,4},{3,1},{4,6},{5,3},{6,8},{7,5},{8,10},{9,7},{10,... | collective-permute-start | bytes 1572872 | tf_op jit(solution)/shard_map/ppermute | solution.py:33
  50.9 3.9 %collective-permute-start.13 = (f32[64,256]{1,0:T(8,128)S(1)}, f32[64,256]{1,0:T(8,128)S(1)}, u32[]{:S(2)}, u32[]{:S(2)}) collective-permute-start(f32[64,256]{1,0:T(8,128)S(1)} %get-tuple-element.49), channel_id=1, source_target_pairs={{0,1},{1,0},{2,3},{3,2},{4,5},{5,4},{6,7},{7,6},{8,9},{9,8},{10,11... | collective-permute-start | bytes 196616 | tf_op jit(solution)/shard_map/ppermute | solution.py:33
  54.8 6.3 %copy-start.1 = (f32[1072,128]{1,0:T(8,128)S(1)}, f32[1072,128]{1,0:T(8,128)}, u32[]{:S(2)}) copy-start(f32[1072,128]{1,0:T(8,128)} %shard_map.88.aux) | copy-start | bytes 1646596
  54.8 6.3 %copy-start.2 = (bf16[1,1024,1664]{2,1,0:T(8,128)(2,1)S(1)}, bf16[1,1024,1664]{2,1,0:T(8,128)(2,1)}, u32[]{:S(2)}) copy-start(bf16[1,1024,1664]{2,1,0:T(8,128)(2,1)} %refs_1_.1) | copy-start | bytes 10223620
  54.9 6.3 %copy-start.4 = (s32[1,16,26]{2,1,0:T(8,128)S(1)}, s32[1,16,26]{2,1,0:T(8,128)}, u32[]{:S(2)}) copy-start(s32[1,16,26]{2,1,0:T(8,128)} %refs_0_.1) | copy-start | bytes 4996
  54.9 16.6 %collective-permute-start.14 = (f32[96,256]{1,0:T(8,128)S(1)}, f32[96,256]{1,0:T(8,128)S(1)}, u32[]{:S(2)}, u32[]{:S(2)}) collective-permute-start(f32[96,256]{1,0:T(8,128)S(1)} %get-tuple-element.51), channel_id=1, source_target_pairs={{0,4},{1,5},{2,6},{3,7},{4,0},{5,1},{6,2},{7,3},{8,12},{9,13},{10,... | collective-permute-start | bytes 294920 | tf_op jit(solution)/shard_map/ppermute | solution.py:33
  66.4 7.4 %collective-permute-start.11 = (f32[64,256]{1,0:T(8,128)S(1)}, f32[64,256]{1,0:T(8,128)S(1)}, u32[]{:S(2)}, u32[]{:S(2)}) collective-permute-start(f32[64,256]{1,0:T(8,128)S(1)} %get-tuple-element.46), channel_id=1, source_target_pairs={{0,2},{1,3},{2,0},{3,1},{4,6},{5,7},{6,4},{7,5},{8,10},{9,11},{10,... | collective-permute-start | bytes 196616 | tf_op jit(solution)/shard_map/ppermute | solution.py:33
  73.8 17.1 %collective-permute-start.16 = (f32[80,256]{1,0:T(8,128)S(1)}, f32[80,256]{1,0:T(8,128)S(1)}, u32[]{:S(2)}, u32[]{:S(2)}) collective-permute-start(f32[80,256]{1,0:T(8,128)S(1)} %get-tuple-element.55), channel_id=1, source_target_pairs={{0,8},{1,9},{2,10},{3,11},{4,12},{5,13},{6,14},{7,15},{8,0},{9,1},... | collective-permute-start | bytes 245768 | tf_op jit(solution)/shard_map/ppermute | solution.py:33
  81.3 7.2 %collective-permute-start.15 = (f32[64,256]{1,0:T(8,128)S(1)}, f32[64,256]{1,0:T(8,128)S(1)}, u32[]{:S(2)}, u32[]{:S(2)}) collective-permute-start(f32[64,256]{1,0:T(8,128)S(1)} %get-tuple-element.54), channel_id=1, source_target_pairs={{4,0},{5,1},{6,2},{7,3},{16,20},{17,21},{18,22},{19,23},{44,40},{4... | collective-permute-start | bytes 196616 | tf_op jit(solution)/shard_map/ppermute | solution.py:33
  82.6 8.3 %collective-permute-start.17 = (f32[64,256]{1,0:T(8,128)S(1)}, f32[64,256]{1,0:T(8,128)S(1)}, u32[]{:S(2)}, u32[]{:S(2)}) collective-permute-start(f32[64,256]{1,0:T(8,128)S(1)} %get-tuple-element.54), channel_id=1, source_target_pairs={{12,0},{13,1},{14,2},{15,3},{24,20},{25,21},{26,22},{27,23},{36,40... | collective-permute-start | bytes 196616 | tf_op jit(solution)/shard_map/ppermute | solution.py:33

commit v5 on v4

--- a/solution.py
+++ b/solution.py
@@ -260,7 +260,8 @@
     term = group ^ (lax.axis_index("leaf") % 4)
     own = kept[...] + came[...]
     early = early_kept[0:64, :] + early_came[0:64, :]
-    total[...] = own
+    total[0:64, :] = own
+    total[64:88, :] = own[0:24, :]
     zero = jnp.zeros_like(own)
     pay[0:64, :] = jnp.where(term == 2, own, jnp.where(term == 1, zero, early))
     base[...] = jnp.where(term == 0, own, jnp.where(term == 3, zero, early))
@@ -272,7 +273,7 @@
 
 
 def last_kernel(base, mass_base, one, two, three, kred, mred):
-    kred[...] = base[...] + one[...] + two[0:64, :] + three[...]
+    kred[...] = base[...] + one[0:64, :] + two[0:64, :] + three[0:64, :]
     mred[...] = mass_base[...] + two[64:80, :]
 
 
@@ -351,7 +352,7 @@
     came = send(go, to_side)
     total, pay, base, mass_base = call(
         gather_kernel,
-        [shape(64, 256), shape(80, 256), shape(64, 256), shape(16, 256)],
+        [shape(88, 256), shape(80, 256), shape(64, 256), shape(16, 256)],
         [keep, came, early_keep, early_came],
     )
     one = send(total, to_own_group(1))

time: 92.2 us -> 94 us (1.020)
  the two profiles are of different devices: /device:TPU:6 before, /device:TPU:144 now
where the time goes in v5:
time: 94 us; the launch traced here: 93.4 us
  starting transfers between devices  57.5 us (61%)
  waiting for transfers between devices  21.5 us (23%)
  Pallas kernels  11.3 us (12%)
  local copies, waits for them, and re-layouts  2.09 us (2%)
    ppermute x18, starting transfers between devices, send(): return lax.ppermute(value, ('leaf', 'rows'), pairs)  57.5 us
    ppermute x18, waiting for transfers between devices, send(): return lax.ppermute(value, ('leaf', 'rows'), pairs)  21.5 us
    pallas_call x11, Pallas kernels, call(): pl.pallas_call(body, out_shape=outs, in_specs=[VMEM] * len(arrays) + [HBM...  11.3 us
    unnamed x10, local copies, waits for them, and re-layouts  2.09 us
  transfers between devices with their start and end apart: 18, of which 7 were waited for; matrix products, arithmetic and copies ran while one was open for 0% of the time, Pallas kernels for 11%

profile of v5, /device:TPU:144, one launch (start us, length us, event | category | flops | bytes accessed | tf_op | source)
XLA Modules:
  0.0 93.4 jit_solution(2807599727511886820)
XLA Ops:
  0.6 1.9 %collective-permute-start = (bf16[1024,256]{1,0:T(8,128)(2,1)}, bf16[1024,256]{1,0:T(8,128)(2,1)S(1)}, u32[]{:S(2)}, u32[]{:S(2)}) collective-permute-start(bf16[1024,256]{1,0:T(8,128)(2,1)} %bitcast.10), channel_id=1, source_target_pairs={{0,1},{1,0},{2,3},{3,2},{4,5},{5,4},{6,7},{7,6},{8,9},{9,8},{10,11... | collective-permute-start | bytes 1572872 | tf_op jit(solution)/shard_map/ppermute | solution.py:33
  2.6 2.4 %collective-permute-start.1 = (bf16[1024,1664]{1,0:T(8,128)(2,1)}, bf16[1024,1664]{1,0:T(8,128)(2,1)S(1)}, u32[]{:S(2)}, u32[]{:S(2)}) collective-permute-start(bf16[1024,1664]{1,0:T(8,128)(2,1)} %bitcast.9), channel_id=1, source_target_pairs={{0,1},{1,0},{2,3},{3,2},{4,5},{5,4},{6,7},{7,6},{8,9},{9,8},{10,11... | collective-permute-start | bytes 10223624 | tf_op jit(solution)/shard_map/ppermute | solution.py:33
  6.7 3.5 %collective-permute-start.3 = (bf16[2048,128]{1,0:T(8,128)(2,1)S(1)}, bf16[2048,128]{1,0:T(8,128)(2,1)S(1)}, u32[]{:S(2)}, u32[]{:S(2)}) collective-permute-start(bf16[2048,128]{1,0:T(8,128)(2,1)S(1)} %get-tuple-element.35.refs_3_), channel_id=1, source_target_pairs={{0,2},{1,15},{2,4},{3,1},{4,6},{5,3},{6,8},{7,5},{8,10},{9,7},{10,... | collective-permute-start | bytes 1572872 | tf_op jit(solution)/shard_map/ppermute | solution.py:33
  10.2 4.3 %collective-permute-start.8 = (bf16[2048,256]{1,0:T(8,128)(2,1)S(1)}, bf16[2048,256]{1,0:T(8,128)(2,1)S(1)}, u32[]{:S(2)}, u32[]{:S(2)}) collective-permute-start(bf16[2048,256]{1,0:T(8,128)(2,1)S(1)} %get-tuple-element.32.both), channel_id=1, source_target_pairs={{0,16},{1,33},{2,18},{3,35},{4,20},{5,37},{6,22},{7,39},{8,24},{9,... | collective-permute-start | bytes 3145736 | tf_op jit(solution)/shard_map/ppermute | solution.py:33
  14.4 2.4 %collective-permute-start.4 = (bf16[2048,128]{1,0:T(8,128)(2,1)S(1)}, bf16[2048,128]{1,0:T(8,128)(2,1)S(1)}, u32[]{:S(2)}, u32[]{:S(2)}) collective-permute-start(bf16[2048,128]{1,0:T(8,128)(2,1)S(1)} %get-tuple-element.35.refs_3_), channel_id=1, source_target_pairs={{0,14},{1,3},{2,0},{3,5},{4,2},{5,7},{6,4},{7,9},{8,6},{9,11},{10,... | collective-permute-start | bytes 1572872 | tf_op jit(solution)/shard_map/ppermute | solution.py:33
  16.8 2.5 %collective-permute-done.3.refs_4_ = bf16[2048,128]{1,0:T(8,128)(2,1)S(1)} collective-permute-done((bf16[2048,128]{1,0:T(8,128)(2,1)S(1)}, bf16[2048,128]{1,0:T(8,128)(2,1)S(1)}, u32[]{:S(2)}, u32[]{:S(2)}) %collective-permute-start.3) | collective-permute-done | bytes 524320 | tf_op jit(solution)/shard_map/ppermute | solution.py:33
  19.3 4.7 %collective-permute-start.5 = (bf16[2048,128]{1,0:T(8,128)(2,1)S(1)}, bf16[2048,128]{1,0:T(8,128)(2,1)S(1)}, u32[]{:S(2)}, u32[]{:S(2)}) collective-permute-start(bf16[2048,128]{1,0:T(8,128)(2,1)S(1)} %collective-permute-done.3.refs_4_), channel_id=1, source_target_pairs={{0,2},{1,15},{2,4},{3,1},{4,6},{5,3},{6,8},{7,5},{8,10},{9,7},{10,... | collective-permute-start | bytes 1572872 | tf_op jit(solution)/shard_map/ppermute | solution.py:33
  24.0 1.8 %shard_map.88.aux = f32[1072,128]{1,0:T(8,128)} custom-call(bf16[1,1024,128]{2,1,0:T(8,128)(2,1)} %couple_at.1, s32[1,16,26]{2,1,0:T(8,128)} %refs_0_.1, s32[1,2,16]{2,1,0:T(2,128)} %bitcast.12, f32[1,1024]{1,0:T(1,128)} %shift_at.1, f32[1,1024]{1,0:T(1,128)} %mass_at.1), custom_call_target="tpu_custom_call" | custom-call | bytes 820992 | tf_op jit(solution)/shard_map/pallas_call | solution.py:65
  25.9 1.9 %collective-permute-start.2 = (f32[1072,128]{1,0:T(8,128)}, f32[1072,128]{1,0:T(8,128)S(1)}, u32[]{:S(2)}, u32[]{:S(2)}) collective-permute-start(f32[1072,128]{1,0:T(8,128)} %shard_map.88.aux), channel_id=1, source_target_pairs={{0,1},{1,0},{2,3},{3,2},{4,5},{5,4},{6,7},{7,6},{8,9},{9,8},{10,11... | collective-permute-start | bytes 1646600 | tf_op jit(solution)/shard_map/ppermute | solution.py:33
  27.8 2.6 %collective-permute-done.4.refs_5_ = bf16[2048,128]{1,0:T(8,128)(2,1)S(1)} collective-permute-done((bf16[2048,128]{1,0:T(8,128)(2,1)S(1)}, bf16[2048,128]{1,0:T(8,128)(2,1)S(1)}, u32[]{:S(2)}, u32[]{:S(2)}) %collective-permute-start.4) | collective-permute-done | bytes 524320 | tf_op jit(solution)/shard_map/ppermute | solution.py:33
  30.4 1.9 %collective-permute-start.6 = (bf16[2048,128]{1,0:T(8,128)(2,1)S(1)}, bf16[2048,128]{1,0:T(8,128)(2,1)S(1)}, u32[]{:S(2)}, u32[]{:S(2)}) collective-permute-start(bf16[2048,128]{1,0:T(8,128)(2,1)S(1)} %collective-permute-done.4.refs_5_), channel_id=1, source_target_pairs={{0,14},{1,3},{2,0},{3,5},{4,2},{5,7},{6,4},{7,9},{8,6},{9,11},{10,... | collective-permute-start | bytes 1572872 | tf_op jit(solution)/shard_map/ppermute | solution.py:33
  32.3 5.5 %collective-permute-start.7 = (bf16[2048,128]{1,0:T(8,128)(2,1)S(1)}, bf16[2048,128]{1,0:T(8,128)(2,1)S(1)}, u32[]{:S(2)}, u32[]{:S(2)}) collective-permute-start(bf16[2048,128]{1,0:T(8,128)(2,1)S(1)} %collective-permute-done.5.refs_6_), channel_id=1, source_target_pairs={{0,2},{1,15},{2,4},{3,1},{4,6},{5,3},{6,8},{7,5},{8,10},{9,7},{10,... | collective-permute-start | bytes 1572872 | tf_op jit(solution)/shard_map/ppermute | solution.py:33
  41.8 5.1 %collective-permute-start.12 = (f32[192,256]{1,0:T(8,128)S(1)}, f32[192,256]{1,0:T(8,128)S(1)}, u32[]{:S(2)}, u32[]{:S(2)}) collective-permute-start(f32[192,256]{1,0:T(8,128)S(1)} %get-tuple-element.39), channel_id=1, source_target_pairs={{0,2},{1,3},{2,0},{3,1},{4,6},{5,7},{6,4},{7,5},{8,10},{9,11},{10,... | collective-permute-start | bytes 589832 | tf_op jit(solution)/shard_map/ppermute | solution.py:33
  47.9 1.9 %collective-permute-start.9 = (bf16[2048,128]{1,0:T(8,128)(2,1)S(1)}, bf16[2048,128]{1,0:T(8,128)(2,1)S(1)}, u32[]{:S(2)}, u32[]{:S(2)}) collective-permute-start(bf16[2048,128]{1,0:T(8,128)(2,1)S(1)} %collective-permute-done.6.refs_7_), channel_id=1, source_target_pairs={{0,14},{1,3},{2,0},{3,5},{4,2},{5,7},{6,4},{7,9},{8,6},{9,11},{10,... | collective-permute-start | bytes 1572872 | tf_op jit(solution)/shard_map/ppermute | solution.py:33
  49.8 5.8 %collective-permute-start.10 = (bf16[2048,128]{1,0:T(8,128)(2,1)S(1)}, bf16[2048,128]{1,0:T(8,128)(2,1)S(1)}, u32[]{:S(2)}, u32[]{:S(2)}) collective-permute-start(bf16[2048,128]{1,0:T(8,128)(2,1)S(1)} %collective-permute-done.7.refs_8_), channel_id=1, source_target_pairs={{0,2},{1,15},{2,4},{3,1},{4,6},{5,3},{6,8},{7,5},{8,10},{9,7},{10,... | collective-permute-start | bytes 1572872 | tf_op jit(solution)/shard_map/ppermute | solution.py:33
  55.7 1.9 %collective-permute-start.13 = (f32[64,256]{1,0:T(8,128)S(1)}, f32[64,256]{1,0:T(8,128)S(1)}, u32[]{:S(2)}, u32[]{:S(2)}) collective-permute-start(f32[64,256]{1,0:T(8,128)S(1)} %get-tuple-element.49), channel_id=1, source_target_pairs={{0,1},{1,0},{2,3},{3,2},{4,5},{5,4},{6,7},{7,6},{8,9},{9,8},{10,11... | collective-permute-start | bytes 196616 | tf_op jit(solution)/shard_map/ppermute | solution.py:33
  58.9 2.2 %collective-permute-start.14 = (f32[96,256]{1,0:T(8,128)S(1)}, f32[96,256]{1,0:T(8,128)S(1)}, u32[]{:S(2)}, u32[]{:S(2)}) collective-permute-start(f32[96,256]{1,0:T(8,128)S(1)} %get-tuple-element.51), channel_id=1, source_target_pairs={{0,4},{1,5},{2,6},{3,7},{4,0},{5,1},{6,2},{7,3},{8,12},{9,13},{10,... | collective-permute-start | bytes 294920 | tf_op jit(solution)/shard_map/ppermute | solution.py:33
  61.1 5.3 %collective-permute-done.9.refs_9_ = bf16[2048,128]{1,0:T(8,128)(2,1)S(1)} collective-permute-done((bf16[2048,128]{1,0:T(8,128)(2,1)S(1)}, bf16[2048,128]{1,0:T(8,128)(2,1)S(1)}, u32[]{:S(2)}, u32[]{:S(2)}) %collective-permute-start.9) | collective-permute-done | bytes 524320 | tf_op jit(solution)/shard_map/ppermute | solution.py:33
  67.8 3.8 %shard_map.92 = (f32[64,256]{1,0:T(8,128)S(1)}, f32[64,256]{1,0:T(8,128)S(1)}, bf16[16384,128]{1,0:T(8,128)(2,1)S(1)}) custom-call(bf16[16384,128]{1,0:T(8,128)(2,1)S(1)} %get-tuple-element.41.table, bf16[2048,1664]{1,0:T(8,128)(2,1)S(1)} %get-tuple-element.42.matrix, f32[2048,128]{1,0:T(8,128)S(1)} %get-tuple-element.43.start, ...), custom_call_target="tpu_custom_call", output_to_operand_aliasing={{2}: (0, {})} | custom-call | flops 1073741824 | bytes 17973248 | tf_op jit(solution)/shard_map/pallas_call | solution.py:65
  71.7 4.3 %collective-permute-start.11 = (f32[64,256]{1,0:T(8,128)S(1)}, f32[64,256]{1,0:T(8,128)S(1)}, u32[]{:S(2)}, u32[]{:S(2)}) collective-permute-start(f32[64,256]{1,0:T(8,128)S(1)} %get-tuple-element.46), channel_id=1, source_target_pairs={{0,2},{1,3},{2,0},{3,1},{4,6},{5,7},{6,4},{7,5},{8,10},{9,11},{10,... | collective-permute-start | bytes 196616 | tf_op jit(solution)/shard_map/ppermute | solution.py:33
  76.0 2.2 %collective-permute-done.11.came = f32[64,256]{1,0:T(8,128)S(1)} collective-permute-done((f32[64,256]{1,0:T(8,128)S(1)}, f32[64,256]{1,0:T(8,128)S(1)}, u32[]{:S(2)}, u32[]{:S(2)}) %collective-permute-start.11) | collective-permute-done | bytes 65568 | tf_op jit(solution)/shard_map/ppermute | solution.py:33
  78.9 3.5 %collective-permute-start.17 = (f32[88,256]{1,0:T(8,128)S(1)}, f32[88,256]{1,0:T(8,128)S(1)}, u32[]{:S(2)}, u32[]{:S(2)}) collective-permute-start(f32[88,256]{1,0:T(8,128)S(1)} %get-tuple-element.54), channel_id=1, source_target_pairs={{12,0},{13,1},{14,2},{15,3},{24,20},{25,21},{26,22},{27,23},{36,40... | collective-permute-start | bytes 270344 | tf_op jit(solution)/shard_map/ppermute | solution.py:33
  82.5 3.6 %collective-permute-start.16 = (f32[80,256]{1,0:T(8,128)S(1)}, f32[80,256]{1,0:T(8,128)S(1)}, u32[]{:S(2)}, u32[]{:S(2)}) collective-permute-start(f32[80,256]{1,0:T(8,128)S(1)} %get-tuple-element.55), channel_id=1, source_target_pairs={{0,8},{1,9},{2,10},{3,11},{4,12},{5,13},{6,14},{7,15},{8,0},{9,1},... | collective-permute-start | bytes 245768 | tf_op jit(solution)/shard_map/ppermute | solution.py:33
  86.1 6.6 %collective-permute-done.16.two = f32[80,256]{1,0:T(8,128)S(1)} collective-permute-done((f32[80,256]{1,0:T(8,128)S(1)}, f32[80,256]{1,0:T(8,128)S(1)}, u32[]{:S(2)}, u32[]{:S(2)}) %collective-permute-start.16) | collective-permute-done | bytes 81952 | tf_op jit(solution)/shard_map/ppermute | solution.py:33
  (33 shorter events, 10.6 us)
Async XLA Ops:
  0.6 5.7 %collective-permute-start = (bf16[1024,256]{1,0:T(8,128)(2,1)}, bf16[1024,256]{1,0:T(8,128)(2,1)S(1)}, u32[]{:S(2)}, u32[]{:S(2)}) collective-permute-start(bf16[1024,256]{1,0:T(8,128)(2,1)} %bitcast.10), channel_id=1, source_target_pairs={{0,1},{1,0},{2,3},{3,2},{4,5},{5,4},{6,7},{7,6},{8,9},{9,8},{10,11... | collective-permute-start | bytes 1572872 | tf_op jit(solution)/shard_map/ppermute | solution.py:33
  2.6 23.3 %collective-permute-start.1 = (bf16[1024,1664]{1,0:T(8,128)(2,1)}, bf16[1024,1664]{1,0:T(8,128)(2,1)S(1)}, u32[]{:S(2)}, u32[]{:S(2)}) collective-permute-start(bf16[1024,1664]{1,0:T(8,128)(2,1)} %bitcast.9), channel_id=1, source_target_pairs={{0,1},{1,0},{2,3},{3,2},{4,5},{5,4},{6,7},{7,6},{8,9},{9,8},{10,11... | collective-permute-start | bytes 10223624 | tf_op jit(solution)/shard_map/ppermute | solution.py:33
  5.0 1.0 %copy-start.3 = (bf16[1,1024,256]{2,1,0:T(8,128)(2,1)S(1)}, bf16[1,1024,256]{2,1,0:T(8,128)(2,1)}, u32[]{:S(2)}) copy-start(bf16[1,1024,256]{2,1,0:T(8,128)(2,1)} %param.7) | copy-start | bytes 1572868
  6.7 12.7 %collective-permute-start.3 = (bf16[2048,128]{1,0:T(8,128)(2,1)S(1)}, bf16[2048,128]{1,0:T(8,128)(2,1)S(1)}, u32[]{:S(2)}, u32[]{:S(2)}) collective-permute-start(bf16[2048,128]{1,0:T(8,128)(2,1)S(1)} %get-tuple-element.35.refs_3_), channel_id=1, source_target_pairs={{0,2},{1,15},{2,4},{3,1},{4,6},{5,3},{6,8},{7,5},{8,10},{9,7},{10,... | collective-permute-start | bytes 1572872 | tf_op jit(solution)/shard_map/ppermute | solution.py:33
  10.2 29.8 %collective-permute-start.8 = (bf16[2048,256]{1,0:T(8,128)(2,1)S(1)}, bf16[2048,256]{1,0:T(8,128)(2,1)S(1)}, u32[]{:S(2)}, u32[]{:S(2)}) collective-permute-start(bf16[2048,256]{1,0:T(8,128)(2,1)S(1)} %get-tuple-element.32.both), channel_id=1, source_target_pairs={{0,16},{1,33},{2,18},{3,35},{4,20},{5,37},{6,22},{7,39},{8,24},{9,... | collective-permute-start | bytes 3145736 | tf_op jit(solution)/shard_map/ppermute | solution.py:33
  14.4 16.0 %collective-permute-start.4 = (bf16[2048,128]{1,0:T(8,128)(2,1)S(1)}, bf16[2048,128]{1,0:T(8,128)(2,1)S(1)}, u32[]{:S(2)}, u32[]{:S(2)}) collective-permute-start(bf16[2048,128]{1,0:T(8,128)(2,1)S(1)} %get-tuple-element.35.refs_3_), channel_id=1, source_target_pairs={{0,14},{1,3},{2,0},{3,5},{4,2},{5,7},{6,4},{7,9},{8,6},{9,11},{10,... | collective-permute-start | bytes 1572872 | tf_op jit(solution)/shard_map/ppermute | solution.py:33
  19.3 13.0 %collective-permute-start.5 = (bf16[2048,128]{1,0:T(8,128)(2,1)S(1)}, bf16[2048,128]{1,0:T(8,128)(2,1)S(1)}, u32[]{:S(2)}, u32[]{:S(2)}) collective-permute-start(bf16[2048,128]{1,0:T(8,128)(2,1)S(1)} %collective-permute-done.3.refs_4_), channel_id=1, source_target_pairs={{0,2},{1,15},{2,4},{3,1},{4,6},{5,3},{6,8},{7,5},{8,10},{9,7},{10,... | collective-permute-start | bytes 1572872 | tf_op jit(solution)/shard_map/ppermute | solution.py:33
  25.9 11.9 %collective-permute-start.2 = (f32[1072,128]{1,0:T(8,128)}, f32[1072,128]{1,0:T(8,128)S(1)}, u32[]{:S(2)}, u32[]{:S(2)}) collective-permute-start(f32[1072,128]{1,0:T(8,128)} %shard_map.88.aux), channel_id=1, source_target_pairs={{0,1},{1,0},{2,3},{3,2},{4,5},{5,4},{6,7},{7,6},{8,9},{9,8},{10,11... | collective-permute-start | bytes 1646600 | tf_op jit(solution)/shard_map/ppermute | solution.py:33
  30.4 17.5 %collective-permute-start.6 = (bf16[2048,128]{1,0:T(8,128)(2,1)S(1)}, bf16[2048,128]{1,0:T(8,128)(2,1)S(1)}, u32[]{:S(2)}, u32[]{:S(2)}) collective-permute-start(bf16[2048,128]{1,0:T(8,128)(2,1)S(1)} %collective-permute-done.4.refs_5_), channel_id=1, source_target_pairs={{0,14},{1,3},{2,0},{3,5},{4,2},{5,7},{6,4},{7,9},{8,6},{9,11},{10,... | collective-permute-start | bytes 1572872 | tf_op jit(solution)/shard_map/ppermute | solution.py:33
  32.3 17.5 %collective-permute-start.7 = (bf16[2048,128]{1,0:T(8,128)(2,1)S(1)}, bf16[2048,128]{1,0:T(8,128)(2,1)S(1)}, u32[]{:S(2)}, u32[]{:S(2)}) collective-permute-start(bf16[2048,128]{1,0:T(8,128)(2,1)S(1)} %collective-permute-done.5.refs_6_), channel_id=1, source_target_pairs={{0,2},{1,15},{2,4},{3,1},{4,6},{5,3},{6,8},{7,5},{8,10},{9,7},{10,... | collective-permute-start | bytes 1572872 | tf_op jit(solution)/shard_map/ppermute | solution.py:33
  37.8 1.1 %copy-start = (f32[1072,128]{1,0:T(8,128)S(1)}, f32[1072,128]{1,0:T(8,128)}, u32[]{:S(2)}) copy-start(f32[1072,128]{1,0:T(8,128)} %shard_map.88.aux) | copy-start | bytes 1646596
  41.8 13.9 %collective-permute-start.12 = (f32[192,256]{1,0:T(8,128)S(1)}, f32[192,256]{1,0:T(8,128)S(1)}, u32[]{:S(2)}, u32[]{:S(2)}) collective-permute-start(f32[192,256]{1,0:T(8,128)S(1)} %get-tuple-element.39), channel_id=1, source_target_pairs={{0,2},{1,3},{2,0},{3,1},{4,6},{5,7},{6,4},{7,5},{8,10},{9,11},{10,... | collective-permute-start | bytes 589832 | tf_op jit(solution)/shard_map/ppermute | solution.py:33
  47.9 18.5 %collective-permute-start.9 = (bf16[2048,128]{1,0:T(8,128)(2,1)S(1)}, bf16[2048,128]{1,0:T(8,128)(2,1)S(1)}, u32[]{:S(2)}, u32[]{:S(2)}) collective-permute-start(bf16[2048,128]{1,0:T(8,128)(2,1)S(1)} %collective-permute-done.6.refs_7_), channel_id=1, source_target_pairs={{0,14},{1,3},{2,0},{3,5},{4,2},{5,7},{6,4},{7,9},{8,6},{9,11},{10,... | collective-permute-start | bytes 1572872 | tf_op jit(solution)/shard_map/ppermute | solution.py:33
  49.8 18.0 %collective-permute-start.10 = (bf16[2048,128]{1,0:T(8,128)(2,1)S(1)}, bf16[2048,128]{1,0:T(8,128)(2,1)S(1)}, u32[]{:S(2)}, u32[]{:S(2)}) collective-permute-start(bf16[2048,128]{1,0:T(8,128)(2,1)S(1)} %collective-permute-done.7.refs_8_), channel_id=1, source_target_pairs={{0,2},{1,15},{2,4},{3,1},{4,6},{5,3},{6,8},{7,5},{8,10},{9,7},{10,... | collective-permute-start | bytes 1572872 | tf_op jit(solution)/shard_map/ppermute | solution.py:33
  55.7 3.1 %collective-permute-start.13 = (f32[64,256]{1,0:T(8,128)S(1)}, f32[64,256]{1,0:T(8,128)S(1)}, u32[]{:S(2)}, u32[]{:S(2)}) collective-permute-start(f32[64,256]{1,0:T(8,128)S(1)} %get-tuple-element.49), channel_id=1, source_target_pairs={{0,1},{1,0},{2,3},{3,2},{4,5},{5,4},{6,7},{7,6},{8,9},{9,8},{10,11... | collective-permute-start | bytes 196616 | tf_op jit(solution)/shard_map/ppermute | solution.py:33
  58.8 7.6 %copy-start.1 = (f32[1072,128]{1,0:T(8,128)S(1)}, f32[1072,128]{1,0:T(8,128)}, u32[]{:S(2)}) copy-start(f32[1072,128]{1,0:T(8,128)} %shard_map.88.aux) | copy-start | bytes 1646596
  58.8 7.6 %copy-start.2 = (bf16[1,1024,1664]{2,1,0:T(8,128)(2,1)S(1)}, bf16[1,1024,1664]{2,1,0:T(8,128)(2,1)}, u32[]{:S(2)}) copy-start(bf16[1,1024,1664]{2,1,0:T(8,128)(2,1)} %refs_1_.1) | copy-start | bytes 10223620
  58.8 7.6 %copy-start.4 = (s32[1,16,26]{2,1,0:T(8,128)S(1)}, s32[1,16,26]{2,1,0:T(8,128)}, u32[]{:S(2)}) copy-start(s32[1,16,26]{2,1,0:T(8,128)} %refs_0_.1) | copy-start | bytes 4996
  58.9 17.1 %collective-permute-start.14 = (f32[96,256]{1,0:T(8,128)S(1)}, f32[96,256]{1,0:T(8,128)S(1)}, u32[]{:S(2)}, u32[]{:S(2)}) collective-permute-start(f32[96,256]{1,0:T(8,128)S(1)} %get-tuple-element.51), channel_id=1, source_target_pairs={{0,4},{1,5},{2,6},{3,7},{4,0},{5,1},{6,2},{7,3},{8,12},{9,13},{10,... | collective-permute-start | bytes 294920 | tf_op jit(solution)/shard_map/ppermute | solution.py:33
  71.7 6.6 %collective-permute-start.11 = (f32[64,256]{1,0:T(8,128)S(1)}, f32[64,256]{1,0:T(8,128)S(1)}, u32[]{:S(2)}, u32[]{:S(2)}) collective-permute-start(f32[64,256]{1,0:T(8,128)S(1)} %get-tuple-element.46), channel_id=1, source_target_pairs={{0,2},{1,3},{2,0},{3,1},{4,6},{5,7},{6,4},{7,5},{8,10},{9,11},{10,... | collective-permute-start | bytes 196616 | tf_op jit(solution)/shard_map/ppermute | solution.py:33
  78.3 14.4 %collective-permute-start.15 = (f32[88,256]{1,0:T(8,128)S(1)}, f32[88,256]{1,0:T(8,128)S(1)}, u32[]{:S(2)}, u32[]{:S(2)}) collective-permute-start(f32[88,256]{1,0:T(8,128)S(1)} %get-tuple-element.54), channel_id=1, source_target_pairs={{4,0},{5,1},{6,2},{7,3},{16,20},{17,21},{18,22},{19,23},{44,40},{4... | collective-permute-start | bytes 270344 | tf_op jit(solution)/shard_map/ppermute | solution.py:33
  78.9 13.8 %collective-permute-start.17 = (f32[88,256]{1,0:T(8,128)S(1)}, f32[88,256]{1,0:T(8,128)S(1)}, u32[]{:S(2)}, u32[]{:S(2)}) collective-permute-start(f32[88,256]{1,0:T(8,128)S(1)} %get-tuple-element.54), channel_id=1, source_target_pairs={{12,0},{13,1},{14,2},{15,3},{24,20},{25,21},{26,22},{27,23},{36,40... | collective-permute-start | bytes 270344 | tf_op jit(solution)/shard_map/ppermute | solution.py:33
  82.5 10.2 %collective-permute-start.16 = (f32[80,256]{1,0:T(8,128)S(1)}, f32[80,256]{1,0:T(8,128)S(1)}, u32[]{:S(2)}, u32[]{:S(2)}) collective-permute-start(f32[80,256]{1,0:T(8,128)S(1)} %get-tuple-element.55), channel_id=1, source_target_pairs={{0,8},{1,9},{2,10},{3,11},{4,12},{5,13},{6,14},{7,15},{8,0},{9,1},... | collective-permute-start | bytes 245768 | tf_op jit(solution)/shard_map/ppermute | solution.py:33
